TPU v7x, 256 devices: a whole 4x4x8 slice. The times are simulated.
256 devices in a mesh: blk: 64 (over y, z, x_lo), sub: 4 (over x_hi, core).
Axes of the slice: x: 4 (x_hi: 2, x_lo: 2; x = x_hi * 2 + x_lo), y: 4, z: 8, core: 2. Of those that a mesh axis runs over, the one named last changes fastest.
Arguments:
- vorticity: float32 [512, 3, 32768], P(('blk', 'sub')), may hold values from -4.5 to 4.5
- velocity: float32 [512, 3, 32768], P(('blk', 'sub')), may hold values from -6 to 6
- level_map: int32 [512], P(('blk', 'sub')), may hold values from 0 to 2
- patch_owner: int32 [512], P(('blk', 'sub')), may hold values from 0 to 255
- neighbours: int32 [512, 6], P(('blk', 'sub')), may hold values from 0 to 23
- fish_slot: int32 [256], P(('blk', 'sub')), may hold values from 0 to 1, as said below
- fish_mask: float32 [256, 32768], P(('blk', 'sub')), may hold values from 0 to 1
- fish_speed: float32 [256, 3], P(('blk', 'sub')), may hold values from -4 to 4
Outputs:
- vorticity_next: float32 [512, 3, 32768], P(('blk', 'sub'))
- velocity_next: float32 [512, 3, 32768], P(('blk', 'sub'))
Inputs may be any that keep to these rules, and one draw needn't show every extreme that they name: `fish_slot`: the 1 entries of one device name distinct slots of that device's 2 blocks.
All inputs are finite; a program needn't handle non-finite values.
Results may differ from a plain program's by a relative error of at most 0.000086.
Values sent between devices are 32-bit elements; how exact they have to be, the bound alone decides.
A program may use at most 192 MiB of HBM per device.

v0:
```python
import math

import jax
import jax.numpy as jnp
from jax import lax
from jax.sharding import PartitionSpec as P

EDGE = 32
GX = 32
GY = 128
GZ = 4
CELLS = 32768
PATCHES = 256


TIME_STEP = 0.05
VISCOSITY = 0.1
PENALTY = 10.0
HIGHEST = lax.Precision.HIGHEST


def extended(cells, sides, width):
    for axis, dim in sides:
        count = lax.axis_size(axis)
        ends = count - 1
        head = lax.slice_in_dim(cells, 0, width, axis=dim)
        tail = lax.slice_in_dim(cells, cells.shape[dim] - width, cells.shape[dim], axis=dim)
        cells = jnp.concatenate(
            [
                lax.ppermute(tail, axis, [(i, (i + 1) % count) for i in range(ends)]),
                cells,
                lax.ppermute(head, axis, [((i + 1) % count, i) for i in range(ends)]),
            ],
            axis=dim,
        )
    return cells


def face_planes(field):
    width = field.shape[0]
    edge = field.shape[1]
    planes = [
        field[:, 0],
        field[:, -1],
        field[:, :, 0],
        field[:, :, -1],
        field[:, :, :, 0],
        field[:, :, :, -1],
    ]
    return jnp.stack([plane.reshape(width, edge * edge) for plane in planes])


def with_ghosts(field, ghosts):
    width = field.shape[0]
    edge = field.shape[1]
    sheet = ghosts.reshape(6, width, edge, edge)
    padded = jnp.pad(field, ((0, 0), (1, 1), (1, 1), (1, 1)))
    padded = padded.at[:, 0, 1:-1, 1:-1].set(sheet[0])
    padded = padded.at[:, -1, 1:-1, 1:-1].set(sheet[1])
    padded = padded.at[:, 1:-1, 0, 1:-1].set(sheet[2])
    padded = padded.at[:, 1:-1, -1, 1:-1].set(sheet[3])
    padded = padded.at[:, 1:-1, 1:-1, 0].set(sheet[4])
    padded = padded.at[:, 1:-1, 1:-1, -1].set(sheet[5])
    return padded


def advance(field, ghosts, level):
    padded = with_ghosts(field, ghosts)
    spacing = jnp.power(0.5, level.astype(jnp.float32))
    centre = padded[:, 1:-1, 1:-1, 1:-1]
    lower = [padded[:, :-2, 1:-1, 1:-1], padded[:, 1:-1, :-2, 1:-1], padded[:, 1:-1, 1:-1, :-2]]
    upper = [padded[:, 2:, 1:-1, 1:-1], padded[:, 1:-1, 2:, 1:-1], padded[:, 1:-1, 1:-1, 2:]]
    slopes = [(upper[which] - lower[which]) / (2.0 * spacing) for which in range(3)]
    vort = centre[:3]
    veloc = centre[3:]
    stretch = vort[0] * slopes[0][3:] + vort[1] * slopes[1][3:] + vort[2] * slopes[2][3:]
    carried = veloc[0] * slopes[0][:3] + veloc[1] * slopes[1][:3] + veloc[2] * slopes[2][:3]
    beside_all = (
        upper[0][:3] + lower[0][:3] + upper[1][:3] + lower[1][:3] + upper[2][:3] + lower[2][:3]
    )
    laplace = (beside_all - 6.0 * vort) / (spacing * spacing)
    return vort + TIME_STEP * (stretch - carried + VISCOSITY * laplace)


def restrict(vort, level):
    edge = vort.shape[1]
    ratio = edge // 4
    cubes = vort.reshape(3, 4, ratio, 4, ratio, 4, ratio)
    return jnp.mean(cubes, axis=(2, 4, 6)) * jnp.power(0.125, level.astype(jnp.float32))


def to_grid(columns):
    parts = columns.reshape(3, 4, 4, 4, GX // 4, GY // 4, GZ // 4)
    return parts.transpose(0, 6, 3, 4, 1, 5, 2).reshape(3, GZ, GX, GY)


def from_grid(grid):
    parts = grid.reshape(3, GZ // 4, 4, GX // 4, 4, GY // 4, 4)
    return parts.transpose(0, 4, 6, 2, 3, 5, 1).reshape(3, 4, 4, 4, PATCHES)


def waves(count, length, first):
    index = jnp.arange(count, dtype=jnp.int32) + first
    signed = jnp.where(index < (length + 1) // 2, index, index - length).astype(jnp.float32)
    full = signed * (2.0 * math.pi / length)
    slope = jnp.where(index == length // 2, 0.0, full)
    return (full, slope)


def biot_savart(real_part, imag_part, yfirst):
    count_z, count_x, count_y = real_part.shape[1:]
    full_z, slope_z = waves(count_z, GZ, 0)
    full_x, slope_x = waves(count_x, GX, 0)
    full_y, slope_y = waves(count_y, GY, yfirst)
    square = full_z[:, None, None] ** 2 + full_x[None, :, None] ** 2 + full_y[None, None, :] ** 2
    inverse_sq = jnp.where(square > 0, 1.0 / jnp.where(square > 0, square, 1.0), 0.0)
    slope_z = slope_z[:, None, None]
    slope_x = slope_x[None, :, None]
    slope_y = slope_y[None, None, :]

    def cross(spectrum):
        psi_x = spectrum[0] * inverse_sq
        psi_y = spectrum[1] * inverse_sq
        psi_z = spectrum[2] * inverse_sq
        return jnp.stack(
            [
                slope_y * psi_z - slope_z * psi_y,
                slope_z * psi_x - slope_x * psi_z,
                slope_x * psi_y - slope_y * psi_x,
            ]
        )

    cross_real = cross(real_part)
    cross_imag = cross(imag_part)
    return (-cross_imag, cross_real)


def dft_tables(length):
    rows_index = jnp.arange(length, dtype=jnp.int32)[:, None]
    cols_index = jnp.arange(length, dtype=jnp.int32)[None, :]
    angle = (rows_index * cols_index % length).astype(jnp.float32) * (2.0 * math.pi / length)
    return (jnp.cos(angle), jnp.sin(angle))


def along(values, matrix, which):
    moved = jnp.tensordot(matrix, values, axes=((1,), (which,)), precision=HIGHEST)
    return jnp.moveaxis(moved, 0, which)


def forward(real_part, imag_part, which):
    cosine, sine = dft_tables(real_part.shape[which])
    if imag_part is None:
        return (along(real_part, cosine, which), -along(real_part, sine, which))
    real_out = along(real_part, cosine, which) + along(imag_part, sine, which)
    imag_out = along(imag_part, cosine, which) - along(real_part, sine, which)
    return (real_out, imag_out)


def inverse(real_part, imag_part, which):
    length = real_part.shape[which]
    cosine, sine = dft_tables(length)
    real_out = (along(real_part, cosine, which) - along(imag_part, sine, which)) / length
    imag_out = (along(imag_part, cosine, which) + along(real_part, sine, which)) / length
    return (real_out, imag_out)


def whole_solve(source_grid):
    real_part, imag_part = forward(source_grid, None, 3)
    real_part, imag_part = forward(real_part, imag_part, 1)
    real_part, imag_part = forward(real_part, imag_part, 2)
    real_part, imag_part = biot_savart(real_part, imag_part, 0)
    real_part, imag_part = inverse(real_part, imag_part, 2)
    real_part, imag_part = inverse(real_part, imag_part, 1)
    solved, _ = inverse(real_part, imag_part, 3)
    return solved


def local_grid(restricted, patch_owner):
    onehot = (patch_owner[:, None] == jnp.arange(PATCHES, dtype=jnp.int32)[None, :]).astype(
        jnp.float32
    )
    columns = jnp.dot(restricted.T, onehot, precision=HIGHEST, preferred_element_type=jnp.float32)
    return to_grid(columns)


def upsample(patch, ratio):
    large = jnp.broadcast_to(patch[:, :, None, :, None, :, None], (3, 4, ratio, 4, ratio, 4, ratio))
    return large.reshape(3, 64 * ratio**3)


def body(vorticity, velocity, level_map, patch_owner, neighbours, fish_slot, fish_mask, fish_speed):
    count = vorticity.shape[0]
    fields = jnp.concatenate([vorticity, velocity], axis=1).reshape(count, 6, EDGE, EDGE, EDGE)
    own_faces = jax.vmap(face_planes)(fields)
    grouped = lax.all_gather(own_faces, "sub", axis=0, tiled=True)
    window = extended(grouped, (("blk", 0),), grouped.shape[0])
    opposite = jnp.bitwise_xor(jnp.arange(6, dtype=jnp.int32), 1)
    flat = neighbours * 6 + opposite[None, :]
    table = window.reshape(-1, 6, EDGE * EDGE)
    ghosts = table[flat]
    fresh = jax.vmap(advance)(fields, ghosts, level_map)
    restricted = jax.vmap(restrict)(fresh, level_map).reshape(count, 192)
    source_grid = lax.psum(local_grid(restricted, patch_owner), ("blk", "sub"))
    coarse_velocity = whole_solve(source_grid)
    patches = jnp.take(from_grid(coarse_velocity), patch_owner, axis=4)
    ratio = EDGE // 4
    lifted = jax.vmap(lambda patch: upsample(patch, ratio))(patches.transpose(4, 0, 1, 2, 3))
    blended = velocity + lifted
    chi = jnp.zeros((count, CELLS), jnp.float32).at[fish_slot].set(fish_mask)
    speed = jnp.zeros((count, 3), jnp.float32).at[fish_slot].set(fish_speed)
    velocity_next = (blended + PENALTY * chi[:, None, :] * speed[:, :, None]) / (
        1.0 + PENALTY * chi[:, None, :]
    )
    return (fresh.reshape(count, 3, CELLS), velocity_next)


def solution(mesh):
    placed = (
        P(("blk", "sub"), None, None),
        P(("blk", "sub"), None, None),
        P(("blk", "sub")),
        P(("blk", "sub")),
        P(("blk", "sub"), None),
        P(("blk", "sub")),
        P(("blk", "sub"), None),
        P(("blk", "sub"), None),
    )
    return jax.shard_map(
        body,
        mesh=mesh,
        in_specs=placed,
        out_specs=(P(("blk", "sub"), None, None), P(("blk", "sub"), None, None)),
        check_vma=False,
    )
```

profile of v0, /device:TPU:1, one launch (start us, length us, event | category | flops | bytes accessed | tf_op | source)
XLA Modules:
  0.0 1037.2 jit_solution(14812033724527119607)
XLA Ops:
  9.3 5.0 reshape.498
  17.6 9.6 slice_reduce_fusion
  33.9 8.0 copy.245
  41.9 8.3 pad.32
  52.5 7.1 all-gather.2.cloned.1.call-done
  63.1 4.1 collective-permute-start
  69.1 47.2 %collective-permute-done.1 = f32[8,6,6,1024]{3,0,2,1:T(8,128)S(1)} collective-permute-done((f32[8,6,6,1024]{3,0,2,1:T(8,128)S(1)}, f32[8,6,6,1024]{3,0,2,1:T(8,128)S(1)}, u32[]{:S(2)}, u32[]{:S(2)}) %collective-permute-start.1) | collective-permute-done | bytes 1179680 | tf_op jit(solution)/shard_map/ppermute | solution.py:32
  124.1 6.2 copy.261
  130.4 6.2 copy.262
  136.5 66.7 %scatter.26 = f32[2,6,34,34,34]{3,2,1,0,4:T(8,128)} dynamic-update-slice(f32[2,6,34,34,34]{3,2,1,0,4:T(8,128)} %pad.32, f32[2,6,1,32,32]{3,2,1,0,4:T(1,128)S(1)} %copy.259, s32[]{:T(128)} %constant.347.clone.1, s32[]{:T(128)} %constant.347.clone.1, s32[]{:T(128)} %constant.347.clone.1, s32[]{:T(128)} %constant.346.clone.1, s32[]{:T(128)} %constant.346.clone.1) | dynamic-update-slice | bytes 98308 | tf_op jit(solution)/shard_map/vmap()/scatter | solution.py:58
  203.2 66.7 %scatter.29 = f32[2,6,34,34,34]{3,2,1,0,4:T(8,128)} dynamic-update-slice(f32[2,6,34,34,34]{3,2,1,0,4:T(8,128)} %scatter.26, f32[2,6,1,32,32]{3,2,1,0,4:T(1,128)S(1)} %copy.260, s32[]{:T(128)} %constant.347.clone.1, s32[]{:T(128)} %constant.347.clone.1, s32[]{:T(128)} %constant.349.clone.1, s32[]{:T(128)} %constant.346.clone.1, s32[]{:T(128)} %constant.346.clone.1) | dynamic-update-slice | bytes 98308 | tf_op jit(solution)/shard_map/vmap()/scatter | solution.py:59
  269.9 26.5 %scatter.30 = f32[2,6,34,34,34]{3,2,1,0,4:T(8,128)} dynamic-update-slice(f32[2,6,34,34,34]{3,2,1,0,4:T(8,128)} %scatter.29, f32[2,6,32,1,32]{3,2,1,0,4:T(8,128)} %copy.261, s32[]{:T(128)} %constant.347.clone.1, s32[]{:T(128)} %constant.347.clone.1, s32[]{:T(128)} %constant.346.clone.1, s32[]{:T(128)} %constant.347.clone.1, s32[]{:T(128)} %constant.346.clone.1) | dynamic-update-slice | bytes 98308 | tf_op jit(solution)/shard_map/vmap()/scatter | solution.py:60
  296.4 72.4 %scatter.31 = f32[2,6,34,34,34]{3,2,1,0,4:T(8,128)} dynamic-update-slice(f32[2,6,34,34,34]{3,2,1,0,4:T(8,128)} %scatter.30, f32[2,6,32,1,32]{3,2,1,0,4:T(8,128)} %copy.262, s32[]{:T(128)} %constant.347.clone.1, s32[]{:T(128)} %constant.347.clone.1, s32[]{:T(128)} %constant.346.clone.1, s32[]{:T(128)} %constant.349.clone.1, s32[]{:T(128)} %constant.346.clone.1) | dynamic-update-slice | bytes 98308 | tf_op jit(solution)/shard_map/vmap()/scatter | solution.py:61
  368.8 9.6 copy.263
  378.4 4.3 copy.264
  382.7 4.3 copy.265
  387.0 34.0 %scatter.34 = f32[2,6,34,34,34]{4,3,2,0,1:T(8,128)} dynamic-update-slice(f32[2,6,34,34,34]{4,3,2,0,1:T(8,128)} %copy.263, f32[2,6,32,32,1]{4,3,2,0,1:T(8,128)} %copy.264, s32[]{:T(128)} %constant.347.clone.1, s32[]{:T(128)} %constant.347.clone.1, s32[]{:T(128)} %constant.346.clone.1, s32[]{:T(128)} %constant.346.clone.1, s32[]{:T(128)} %constant.347.clone.1) | dynamic-update-slice | bytes 98308 | tf_op jit(solution)/shard_map/vmap()/scatter | solution.py:62
  421.0 74.5 %scatter.35 = f32[2,6,34,34,34]{4,3,2,0,1:T(8,128)} dynamic-update-slice(f32[2,6,34,34,34]{4,3,2,0,1:T(8,128)} %scatter.34, f32[2,6,32,32,1]{4,3,2,0,1:T(8,128)} %copy.265, s32[]{:T(128)} %constant.347.clone.1, s32[]{:T(128)} %constant.347.clone.1, s32[]{:T(128)} %constant.346.clone.1, s32[]{:T(128)} %constant.346.clone.1, s32[]{:T(128)} %constant.349.clone.1) | dynamic-update-slice | bytes 98308 | tf_op jit(solution)/shard_map/vmap()/scatter | solution.py:63
  495.4 30.6 %fusion.214 = (f32[2,6,32,32,32]{4,3,2,0,1:T(8,128)}, f32[2,6,32,32,32]{4,3,2,0,1:T(8,128)}, f32[2,6,32,32,32]{4,3,2,0,1:T(8,128)}, f32[2,6,32,32,32]{4,3,2,0,1:...) fusion(f32[2,6,34,34,34]{4,3,2,0,1:T(8,128)} %scatter.35), kind=kLoop, calls=%fused_computation.286 | loop fusion | bytes 18874368 | tf_op jit(solution)/shard_map/vmap()/slice | solution.py:71
  526.0 6.7 fusion.213
  532.7 7.6 fusion.212
  540.3 8.0 copy.327
  548.3 8.0 copy.328
  556.3 8.0 copy.330
  564.3 8.0 copy.331
  572.2 8.0 copy.333
  580.2 8.4 copy.334
  602.7 21.1 %subtract_divide_fusion.2 = (f32[2,6,32,32,32]{3,2,1,0,4:T(8,128)}, f32[2,6,32,32,32]{3,2,1,0,4:T(8,128)}, f32[2,6,32,32,32]{3,2,1,0,4:T(8,128)}) fusion(f32[2,6,32,32,32]{3,2,1,0,4:T(8,128)} %copy.327, f32[2,6,32,32,32]{3,2,1,0,4:T(8,128)} %copy.328, f32[2]{0:T(128)S(1)} %get-tuple-element.140, f32[2,6,32,32,32]{3,2,1,0,4:T(8,128)} %copy.330, ...), kind=kLoop, calls=%fused_computation.6 | loop fusion | flops 2359296 | bytes 14155784 | tf_op jit(solution)/shard_map/vmap()/div | solution.py:73
  623.8 10.6 %fusion.7 = f32[2,3,32,32,32]{3,2,1,0,4:T(8,128)S(1)} fusion(f32[2,6,32,32,32]{3,2,1,0,4:T(8,128)} %get-tuple-element.143, f32[2,6,32,32,32]{3,2,1,0,4:T(8,128)} %get-tuple-element.142, f32[2,6,32,32,32]{3,2,1,0,4:T(8,128)} %get-tuple-element.141, f32[2,32,32,32]{2,1,0,3:T(8,128)} %bitcast.170, f32[2,32,32,32]{2,1,0,3:T(8,128)} %bitcast.171, ...), kind=kLoop, calls=%fused_computation.17 | loop fusion | flops 2162688 | bytes 7077888 | tf_op jit(solution)/shard_map/vmap()/sub | solution.py:82
  637.2 4.0 copy.342
  641.2 4.8 copy.341
  646.0 4.9 copy.340
  650.9 4.8 copy.338
  655.7 4.8 copy.339
  660.5 8.3 add_add_fusion
  668.8 4.0 copy.283
  672.7 6.6 fusion.5
  679.3 3.6 copy.285
  682.9 10.0 reshape.508
  692.9 7.1 reduce_sum.11
  702.3 5.3 copy.288
  707.6 7.1 reshape.509
  717.6 243.5 %all-reduce.3.cloned.1.call-done = f32[3,4,32,128]{3,2,1,0:T(8,128)} async-done(((f32[3,4,32,128]{3,2,1,0:T(8,128)}), f32[3,4,32,128]{3,2,1,0:T(8,128)}) %all-reduce.3.cloned.1.call-update) | async-done | bytes 196624 | tf_op jit(solution)/shard_map/psum | solution.py:203
  973.2 7.9 reshape.510
  981.1 21.1 %copy.318 = f32[3,4,4,4,8,32,1]{3,2,5,4,1,0,6:T(4,128)} copy(f32[3,4,4,4,8,32,1]{2,5,1,4,3,0,6:T(8,128)} %bitcast.167) | data formatting | bytes 393216 | tf_op jit(solution)/shard_map/reshape | solution.py:99
  1002.1 3.5 gather_fusion.1
  1005.7 6.3 broadcast_in_dim.42
  1012.0 16.4 %reshape.512 = f32[2,3,32768]{2,0,1:T(2,128)S(1)} reshape(f32[2,3,4,8,4,8,4,8]{7,6,5,4,3,2,0,1:T(4,128)} %broadcast_in_dim.42) | data formatting | bytes 1572864 | tf_op jit(solution)/shard_map/vmap()/reshape | solution.py:188
  (128 shorter events, 62.2 us)
Async XLA Ops:
  7.2 52.4 %all-gather.2.cloned.1.call-start = ((), (), s32[]{:S(2)}) async-start(), calls=%async_computation | async-start | bytes 1966080 | tf_op jit(solution)/shard_map/all_gather | solution.py:195
  27.1 2.6 copy-start.15
  27.2 3.3 copy-start.5
  29.0 932.1 %all-reduce.3.cloned.1.call-start = ((), (), s32[]{:S(2)}) async-start(), calls=%async_computation.1 | async-start | bytes 393216 | tf_op jit(solution)/shard_map/psum | solution.py:203
  41.9 8.3 copy-start.9
  41.9 8.4 copy-start.17
  41.9 25.3 %copy-start.16 = (s32[2]{0:T(128)S(1)}, s32[2]{0:T(128)}, u32[]{:S(2)}) copy-start(s32[2]{0:T(128)} %param.27) | copy-start | bytes 28
  41.9 26.5 %copy-start.14 = (s32[2]{0:T(128)S(1)}, s32[2]{0:T(128)}, u32[]{:S(2)}) copy-start(s32[2]{0:T(128)} %param.26) | copy-start | bytes 28
  51.3 66.4 %copy-start.6 = (f32[2,3]{0,1:T(4,128)}, f32[2,3]{0,1:T(4,128)S(1)}, u32[]{:S(2)}) copy-start(f32[2,3]{0,1:T(4,128)S(1)} %scatter.39) | copy-start | bytes 76
  61.7 56.1 %copy-start.1 = (f32[8,6,6,1024]{3,2,1,0:T(8,128)S(1)}, f32[8,6,6,1024]{3,2,1,0:T(8,128)}, u32[]{:S(2)}) copy-start(f32[8,6,6,1024]{3,2,1,0:T(8,128)} %all-gather.2.cloned.1.call-done) | copy-start | bytes 3538948
  61.7 54.6 %collective-permute-start.1 = (f32[8,6,6,1024]{3,0,2,1:T(8,128)S(1)}, f32[8,6,6,1024]{3,0,2,1:T(8,128)S(1)}, u32[]{:S(2)}, u32[]{:S(2)}) collective-permute-start(f32[8,6,6,1024]{3,0,2,1:T(8,128)S(1)} %copy.253), channel_id=1, source_target_pairs={{4,0},{8,4},{12,8},{16,12},{20,16},{24,20},{28,24},{32,28},{36,32}... | collective-permute-start | bytes 3538952 | tf_op jit(solution)/shard_map/ppermute | solution.py:32
  63.1 53.9 %collective-permute-start = (f32[8,6,6,1024]{3,0,2,1:T(8,128)S(1)}, f32[8,6,6,1024]{3,0,2,1:T(8,128)S(1)}, u32[]{:S(2)}, u32[]{:S(2)}) collective-permute-start(f32[8,6,6,1024]{3,0,2,1:T(8,128)S(1)} %copy.253), channel_id=1, source_target_pairs={{0,4},{4,8},{8,12},{12,16},{16,20},{20,24},{24,28},{28,32},{32,36}... | collective-permute-start | bytes 3538952 | tf_op jit(solution)/shard_map/ppermute | solution.py:30
  526.0 6.7 copy-start
  717.5 250.4 %copy-start.8 = (f32[4,32]{1,0:T(4,128)S(1)}, f32[4,32]{1,0:T(4,128)}, u32[]{:S(2)}) copy-start(f32[4,32]{1,0:T(4,128)} %broadcast_add_fusion) | copy-start | bytes 1540
  717.5 250.4 %copy-start.11 = (f32[4]{0:T(128)S(1)}, f32[4]{0:T(128)}, u32[]{:S(2)}) copy-start(f32[4]{0:T(128)} %compare_select_fusion.6) | copy-start | bytes 52
  717.5 250.4 %copy-start.12 = (f32[128]{0:T(128)S(1)}, f32[128]{0:T(128)}, u32[]{:S(2)}) copy-start(f32[128]{0:T(128)} %get-tuple-element.144) | copy-start | bytes 1540
  717.6 250.4 %copy-start.13 = (f32[128]{0:T(128)S(1)}, f32[128]{0:T(128)}, u32[]{:S(2)}) copy-start(f32[128]{0:T(128)} %get-tuple-element.145) | copy-start | bytes 1540
  981.1 24.6 %copy-start.10 = (pred[2]{0:T(512)(128)(4,1)S(1)}, pred[2]{0:T(512)(128)(4,1)}, u32[]{:S(2)}) copy-start(pred[2]{0:T(512)(128)(4,1)} %compare_and_fusion) | copy-start | bytes 10
  1012.0 16.5 %copy-start.2 = (f32[2,3,32768]{2,0,1:T(2,128)S(1)}, f32[2,3,32768]{2,0,1:T(2,128)}, u32[]{:S(2)}) copy-start(f32[2,3,32768]{2,0,1:T(2,128)} %param.25) | copy-start | bytes 2359300
  1012.0 16.5 %copy-start.3 = (f32[2,32768]{1,0:T(2,128)S(1)}, f32[2,32768]{1,0:T(2,128)}, u32[]{:S(2)}) copy-start(f32[2,32768]{1,0:T(2,128)} %get-tuple-element.127) | copy-start | bytes 786436
  1012.0 16.5 %copy-start.4 = (f32[2,32768]{1,0:T(2,128)S(1)}, f32[2,32768]{1,0:T(2,128)}, u32[]{:S(2)}) copy-start(f32[2,32768]{1,0:T(2,128)} %get-tuple-element.128) | copy-start | bytes 786436
  1012.0 16.5 %copy-start.7 = (f32[2,3]{0,1:T(4,128)S(1)}, f32[2,3]{0,1:T(4,128)}, u32[]{:S(2)}) copy-start(f32[2,3]{0,1:T(4,128)} %copy-done.6) | copy-start | bytes 76
Sparse Core Ops, SparseCore 0:
  29.1 30.4 all-gather.1
  714.9 246.1 all-reduce.2
where the time goes:
time: 1050 us; the launch traced here: 1040 us
  local copies, waits for them, and re-layouts  638 us (61%)
  waiting for transfers between devices  298 us (28%)
  other arithmetic  66.3 us (6%)
  between operations  15.8 us (2%)
  matrix products  13.5 us (1%)
    psum x1, waiting for transfers between devices, body(): source_grid = lax.psum(local_grid(restricted, patch_owner), ('blk', 'sub'))  243 us
    unnamed x59, local copies, waits for them, and re-layouts  86.8 us
    scatter x2, local copies, waits for them, and re-layouts, with_ghosts(): padded = padded.at[:, 1:-1, -1, 1:-1].set(sheet[3])  82 us
    scatter x1, local copies, waits for them, and re-layouts, with_ghosts(): padded = padded.at[:, 1:-1, 1:-1, -1].set(sheet[5])  74.5 us
    scatter x1, local copies, waits for them, and re-layouts, with_ghosts(): padded = padded.at[:, -1, 1:-1, 1:-1].set(sheet[1])  66.7 us
    scatter x1, local copies, waits for them, and re-layouts, with_ghosts(): padded = padded.at[:, 0, 1:-1, 1:-1].set(sheet[0])  66.7 us
    ppermute x1, waiting for transfers between devices, extended(): lax.ppermute(head, axis, [((i + 1) % count, i) for i in range(ends)])  47.2 us
    scatter x1, local copies, waits for them, and re-layouts, with_ghosts(): padded = padded.at[:, 1:-1, 1:-1, 0].set(sheet[4])  34 us
  transfers between devices with their start and end apart: 4, of which 3 were waited for; matrix products, arithmetic and copies ran while one was open for 3% of the time, Pallas kernels for 0%

commit v1 on v0

v1 whole, which is shorter than its diff:
```python
import functools
import math

import jax
import jax.numpy as jnp
import numpy as np
from jax import lax
from jax.experimental import pallas as pl
from jax.experimental.pallas import tpu as pltpu
from jax.sharding import PartitionSpec as P

MESH = pl.DeviceIdType.MESH
HIGHEST = lax.Precision.HIGHEST
RINGS = 32
GX = 32
GY = 128
GZ = 4


def dft_tables():
    space = np.arange(128)
    px, ix, iz = space // 16, (space // 4) % 4, space % 4
    x, z = 4 * px + ix, iz
    kx, kz = space // 4, space % 4
    iy, py = space // 32, space % 32
    y = 4 * py + iy
    ky = space
    theta = 2.0 * np.pi * ((kx[:, None] * x[None, :] % 32) / 32.0 + (kz[:, None] * z[None, :] % 4) / 4.0)
    phi = 2.0 * np.pi * ((y[:, None] * ky[None, :]) % 128) / 128.0
    fwd_y = np.concatenate([np.cos(phi), -np.sin(phi)], axis=1)
    fwd_xz = np.concatenate([np.cos(theta), np.sin(theta)], axis=0)
    inv_xz = np.concatenate([np.cos(theta.T), np.sin(theta.T)], axis=0)
    inv_y = np.concatenate([np.cos(phi.T), -np.sin(phi.T)], axis=0) / 16384.0

    def waves(index, length):
        signed = np.where(index < (length + 1) // 2, index, index - length)
        full = signed * (2.0 * math.pi / length)
        return full, np.where(index == length // 2, 0.0, full)

    full_x, slope_x = waves(kx, GX)
    full_y, slope_y = waves(ky, GY)
    full_z, slope_z = waves(kz, GZ)
    square = (full_x**2 + full_z**2)[:, None] + (full_y**2)[None, :]
    inverse = np.where(square > 0, 1.0 / np.where(square > 0, square, 1.0), 0.0)
    one = np.ones((128, 128))
    spectral = np.concatenate([inverse, slope_x[:, None] * one, slope_y[None, :] * one, slope_z[:, None] * one])
    return tuple(a.astype(np.float32) for a in (fwd_y, fwd_xz, inv_xz, inv_y, spectral))


def fold_tables():
    row = np.arange(192)
    lane = np.arange(128)
    n = np.arange(256)
    row_c_ix, row_iy, row_b = row // 16, (row % 16) // 4, row % 2
    lane_iz = (lane % 32) // 8
    live = n < 192
    fold = ((lane_iz[:, None] == n[None, :] % 4) & live[None, :]) * 1.0
    pick = ((n[None, :] // 4 == (row_iy * 12 + row_c_ix)[:, None]) & live[None, :]) * 1.0
    mean = (np.arange(8)[:, None] == row_b[None, :]) / 512.0
    src = np.arange(96)
    src_c, src_b, src_ix, src_iz = src // 32, (src // 16) % 2, (src // 4) % 4, src % 4
    spread_y = (lane[None, :] // 32 == row_iy[:, None]) * 1.0
    match = ((src_c * 4 + src_ix)[None, :] == row_c_ix[:, None]) & (src_b[None, :] == row_b[:, None])
    spread_z = (src_iz[:, None] == lane_iz[None, :]) * 1.0
    return tuple(a.astype(np.float32) for a in (fold, pick, mean, spread_y, match * 1.0, spread_z))


def iota(shape, dim):
    return lax.broadcasted_iota(jnp.int32, shape, dim)


def place():
    blk, sub = lax.axis_index("blk"), lax.axis_index("sub")
    return blk // 2, lax.rem(blk, 2), sub


def faces_kernel(nb_ref, w_ref, u_ref, out_ref, s1, r1, s2, r2, tmp, nbs, nbr, ssem, rsem):
    ring, half, sub = place()
    me = half * 4 + sub

    def mate(k):
        other = lax.bitwise_xor(me, k)
        return (ring * 2 + other // 4, lax.rem(other, 4))

    def beside(step):
        return (lax.rem(ring + step + RINGS, RINGS) * 2 + half, sub)

    barrier = pltpu.get_barrier_semaphore()
    for k in range(1, 8):
        pl.semaphore_signal(barrier, inc=1, device_id=mate(k), device_id_type=MESH)
    for step in (-1, 1):
        pl.semaphore_signal(barrier, inc=1, device_id=beside(step), device_id_type=MESH)

    lane = iota((8, 128), 1)
    row = iota((8, 128), 0)
    wants = jnp.zeros((8, 128), jnp.int32)
    for b in range(2):
        for f in range(6):
            wants = jnp.where(lane == b * 6 + f, nb_ref[b, f] + half * 8, wants)
    nbs[...] = wants
    nbr[pl.ds(pl.multiple_of(me * 8, 8), 8), :] = wants

    def source(c):
        return (w_ref, u_ref)[c // 3], (c % 3) * 512

    def put(b, f, c, plane):
        s1[pl.ds((b * 6 + f) * 6 + c, 8, stride=72), :] = plane

    for c in range(6):
        ref, base = source(c)
        for b in range(2):
            for f, x in ((0, 0), (1, 31)):
                put(b, f, c, ref[pl.ds(base + x * 16 + b, 8, stride=2), :])
            low = high = jnp.zeros((8, 128), jnp.float32)
            for g in range(4):
                first = ref[pl.ds(base + g * 128 + b, 8, stride=16), :]
                last = ref[pl.ds(base + g * 128 + 14 + b, 8, stride=16), :]
                if g:
                    first = pltpu.roll(first, 32 * g, 1)
                if g != 3:
                    last = pltpu.roll(last, (32 * g + 32) % 128, 1)
                here = lane // 32 == g
                low = jnp.where(here, first, low)
                high = jnp.where(here, last, high)
            put(b, 2, c, low)
            put(b, 3, c, high)

    def gather_z(x, held):
        at_low = (lane & 31) == x
        at_high = (lane & 31) == ((x + 31) & 31)
        fresh = []
        for c in range(6):
            ref, base = source(c)
            for h in range(2):
                plane = ref[pl.ds(pl.multiple_of(base + x * 16 + h * 8, 8), 8), :]
                turned = pltpu.roll(plane, x, 1)
                low, high = held[(c * 2 + h) * 2], held[(c * 2 + h) * 2 + 1]
                fresh += [jnp.where(at_low, turned, low), jnp.where(at_high, turned, high)]
        return tuple(fresh)

    zero = jnp.zeros((8, 128), jnp.float32)
    packed = lax.fori_loop(0, 32, gather_z, (zero,) * 24)
    for c in range(6):
        for which in range(2):
            for h in range(2):
                at = (c * 2 + which) * 16 + h * 8
                tmp[at : at + 8, :] = packed[(c * 2 + h) * 2 + which]
    for c in range(6):
        for which in range(2):
            for b in range(2):
                put(b, 4 + which, c, tmp[pl.ds((c * 2 + which) * 16 + b, 8, stride=2), :])

    pl.semaphore_wait(barrier, 9)
    copies = []
    for k in range(1, 8):
        at = pl.ds(pl.multiple_of(me * 8, 8), 8)
        copies.append(pltpu.make_async_remote_copy(
            src_ref=nbs, dst_ref=nbr.at[at], send_sem=ssem.at[k], recv_sem=rsem.at[k],
            device_id=mate(k), device_id_type=MESH))
        other = lax.bitwise_xor(me, k)
        copies.append(pltpu.make_async_remote_copy(
            src_ref=s1.at[pl.ds(pl.multiple_of(other * 72, 8), 72)],
            dst_ref=r1.at[pl.ds(pl.multiple_of((4 + me) * 72, 8), 72)],
            send_sem=ssem.at[8 + k], recv_sem=rsem.at[8 + k],
            device_id=mate(k), device_id_type=MESH))
    for copy in copies:
        copy.start()
    r1[pl.ds(pl.multiple_of((4 + me) * 72, 8), 72), :] = s1[pl.ds(pl.multiple_of(me * 72, 8), 72), :]
    for copy in copies:
        copy.wait()

    copies = []
    for which, (src, dst, step) in enumerate(((8, 0, 1), (4, 12, -1))):
        copies.append(pltpu.make_async_remote_copy(
            src_ref=r1.at[pl.ds(src * 72, 288)], dst_ref=r1.at[pl.ds(dst * 72, 288)],
            send_sem=ssem.at[16 + which], recv_sem=rsem.at[16 + which],
            device_id=beside(step), device_id_type=MESH))
    for copy in copies:
        copy.start()
    for copy in copies:
        copy.wait()

    wanted = nbr[pl.ds(0, 8, stride=8), :]
    dead_low = (ring == 0).astype(jnp.int32)
    dead_high = (ring == RINGS - 1).astype(jnp.int32)
    slot = iota((8, 32), 1)
    alive = 1 - dead_low * (slot < 8).astype(jnp.int32) - dead_high * (slot >= 24).astype(jnp.int32)
    alive = alive.astype(jnp.float32)
    for f in range(6):
        hot = jnp.concatenate(
            [jnp.where(wanted[:, b * 6 + f : b * 6 + f + 1] == slot, alive, 0.0) for b in range(2)], axis=0)
        data = jnp.concatenate(
            [r1[pl.ds((f ^ 1) * 6 + c, 32, stride=36), :] for c in range(6)], axis=1)
        got = jnp.dot(hot, data, precision=HIGHEST, preferred_element_type=jnp.float32)
        for b in range(2):
            for c in range(6):
                s2[pl.ds((b * 6 + f) * 6 + c, 8, stride=72), :] = got[b * 8 : b * 8 + 8, c * 128 : c * 128 + 128]

    copies = []
    for k in range(1, 8):
        other = lax.bitwise_xor(me, k)
        copies.append(pltpu.make_async_remote_copy(
            src_ref=s2.at[pl.ds(pl.multiple_of(other * 72, 8), 72)],
            dst_ref=r2.at[pl.ds(pl.multiple_of(me * 72, 8), 72)],
            send_sem=ssem.at[18 + k], recv_sem=rsem.at[18 + k],
            device_id=mate(k), device_id_type=MESH))
    for copy in copies:
        copy.start()
    r2[pl.ds(pl.multiple_of(me * 72, 8), 72), :] = s2[pl.ds(pl.multiple_of(me * 72, 8), 72), :]
    for copy in copies:
        copy.wait()
    out_ref[...] = r2[...]


def row_pair(first, second):
    return jnp.where((iota((8, 128), 0) & 1) == 0, first, second)


def stencil_kernel(level_ref, owner_ref, w_ref, u_ref, gh_ref, fold_ref, pick_ref, mean_ref,
                   out_ref, tile_ref, gx, gy, gz, acc):
    lane = iota((8, 128), 1)
    row = iota((8, 128), 0)

    def ghost(b, f, c):
        return gh_ref[pl.ds((b * 6 + f) * 6 + c, 8, stride=72), :]

    for c in range(6):
        for b in range(2):
            for f in range(2):
                gx[pl.ds((f * 6 + c) * 16 + b, 8, stride=2), :] = ghost(b, f, c)
                gz[pl.ds((f * 6 + c) * 16 + b, 8, stride=2), :] = ghost(b, 4 + f, c)
            low, high = ghost(b, 2, c), ghost(b, 3, c)
            for g in range(4):
                at = (c * 32 + g * 8) * 8 + b
                gy[pl.ds(at, 8, stride=8), :] = pltpu.roll(low, 96 - 32 * g, 1) if g != 3 else low
                gy[pl.ds(at + 6, 8, stride=8), :] = pltpu.roll(high, 128 - 32 * g, 1) if g else high
    acc[...] = jnp.zeros_like(acc)

    def scale(level):
        return lax.shift_left(1, level).astype(jnp.float32)

    size = row_pair(scale(level_ref[0]), scale(level_ref[1]))
    slope = (0.05 * 0.5) * size
    spread = (0.05 * 0.1) * (size * size)

    def around(x, c, h):
        ref = (w_ref, u_ref)[c // 3]
        at = (c % 3) * 32 + x
        rows = slice(h * 8, h * 8 + 8)
        here = ref[at, rows, :]
        if isinstance(x, int) and x == 0:
            left = gx[c * 16 + h * 8 : c * 16 + h * 8 + 8, :]
        else:
            left = ref[at - 1, rows, :]
        if isinstance(x, int) and x == 31:
            right = gx[(6 + c) * 16 + h * 8 : (6 + c) * 16 + h * 8 + 8, :]
        else:
            right = ref[at + 1, rows, :]
        side = gy[pl.ds(pl.multiple_of((c * 32 + x) * 8, 8), 8), :]
        if h == 0:
            before = jnp.where(row < 2, side, pltpu.roll(here, 2, 0))
            after = ref[at, 2:10, :]
        else:
            before = ref[at, 6:14, :]
            after = jnp.where(row >= 6, side, pltpu.roll(here, 6, 0))
        before = pltpu.roll(jnp.where(lane >= 96, before, here), 32, 1)
        after = pltpu.roll(jnp.where(lane < 32, after, here), 96, 1)
        below = gz[c * 16 + h * 8 : c * 16 + h * 8 + 8, :]
        above = gz[(6 + c) * 16 + h * 8 : (6 + c) * 16 + h * 8 + 8, :]
        below = jnp.where((lane & 31) == 0, pltpu.roll(below, (97 - x) & 127, 1), pltpu.roll(here, 1, 1))
        above = jnp.where((lane & 31) == 31, pltpu.roll(above, (31 - x) & 127, 1), pltpu.roll(here, 127, 1))
        return here, (left, right), (before, after), (below, above)

    def plane(x):
        for h in range(2):
            parts = [around(x, c, h) for c in range(6)]
            heres = [part[0] for part in parts]
            slopes = [[part[1 + d][1] - part[1 + d][0] for d in range(3)] for part in parts]
            for i in range(3):
                turn = heres[0] * slopes[3 + i][0] + heres[1] * slopes[3 + i][1] + heres[2] * slopes[3 + i][2]
                turn -= heres[3] * slopes[i][0] + heres[4] * slopes[i][1] + heres[5] * slopes[i][2]
                ends = [part for d in range(3) for part in parts[i][1 + d]]
                total = (ends[0] + ends[1]) + (ends[2] + ends[3]) + (ends[4] + ends[5])
                fresh = heres[i] + slope * turn + spread * (total - 6.0 * heres[i])
                out_ref[i * 32 + x, h * 8 : h * 8 + 8, :] = fresh
                at = pl.multiple_of((i * 4 + x // 8) * 16 + h * 8, 8)
                acc[pl.ds(at, 8), :] += fresh

    plane(0)

    def step(x, carry):
        plane(x)
        return carry

    lax.fori_loop(1, 31, step, 0)
    plane(31)

    folded = jnp.dot(acc[...], fold_ref[...], precision=HIGHEST, preferred_element_type=jnp.float32)
    folded = folded * pick_ref[...]
    rows = jnp.dot(mean_ref[...], folded, precision=HIGHEST, preferred_element_type=jnp.float32)
    wide_row, wide_lane = iota((8, 256), 0), iota((8, 256), 1)

    def shrink(level):
        return jnp.where(level == 0, 1.0, jnp.where(level == 1, 0.125, 0.015625))

    rows = rows * jnp.where(wide_row == 0, shrink(level_ref[0]), shrink(level_ref[1]))
    owners = jnp.where(wide_row == 0, owner_ref[0], owner_ref[1]).astype(jnp.float32)
    rows = jnp.where(wide_lane == 192, owners, rows)
    tile_ref[...] = jnp.concatenate(
        [rows[0:1, 0:128], rows[0:1, 128:256], rows[1:2, 0:128], rows[1:2, 128:256], jnp.zeros((4, 128), jnp.float32)],
        axis=0)


def gather_kernel(tile_ref, out_ref, t1, g, ssem, rsem):
    ring, half, sub = place()
    me = half * 4 + sub
    y, z = ring // 8, lax.rem(ring, 8)

    def mate(k):
        other = lax.bitwise_xor(me, k)
        return (ring * 2 + other // 4, lax.rem(other, 4))

    def along_z(k):
        return ((y * 8 + lax.rem(z + k, 8)) * 2 + half, sub)

    def along_y(k):
        return ((lax.rem(y + k, 4) * 8 + z) * 2 + half, sub)

    everyone = [mate(k) for k in range(1, 8)] + [along_z(k) for k in range(1, 8)] + [along_y(k) for k in range(1, 4)]
    barrier = pltpu.get_barrier_semaphore()
    for device in everyone:
        pl.semaphore_signal(barrier, inc=1, device_id=device, device_id_type=MESH)
    pl.semaphore_wait(barrier, len(everyone))

    def spread(ref, targets, first):
        copies = [
            pltpu.make_async_remote_copy(
                src_ref=ref, dst_ref=ref, send_sem=ssem.at[first + n], recv_sem=rsem.at[first + n],
                device_id=device, device_id_type=MESH)
            for n, device in enumerate(targets)
        ]
        for copy in copies:
            copy.start()
        for copy in copies:
            copy.wait()

    mine = pl.ds(pl.multiple_of(me * 8, 8), 8)
    t1[mine, :] = tile_ref[...]
    spread(t1.at[mine], everyone[:7], 0)
    at = pl.ds(pl.multiple_of(ring * 8, 8), 8)
    for t in range(4):
        g[at, t * 128 : t * 128 + 128] = t1[pl.ds(t, 8, stride=8), :]
    spread(g.at[at], everyone[7:14], 7)
    spread(g.at[pl.ds(pl.multiple_of(y * 64, 64), 64)], everyone[14:], 14)
    out_ref[...] = g[...]


def solve_kernel(owner_ref, slot_ref, speed_ref, mask_ref, u_ref, g_ref, fwd_y, fwd_xz, inv_xz, inv_y, spectral,
                 spread_y, match, spread_z, out_ref, chi, field):
    dot = functools.partial(jnp.dot, precision=HIGHEST, preferred_element_type=jnp.float32)
    sent = jnp.concatenate([g_ref[:, 0:256], g_ref[:, 256:512]], axis=0)
    hot = (sent[:, 192:193] == iota((512, 256), 1).astype(jnp.float32)).astype(jnp.float32)
    columns = lax.dot_general(sent, hot, (((0,), (0,)), ((), ())), precision=HIGHEST, preferred_element_type=jnp.float32)
    lane = iota((48, 128), 1)
    rows = []
    for px in range(8):
        held = jnp.zeros((48, 128), jnp.float32)
        for iy in range(4):
            part = columns[iy * 48 : iy * 48 + 48, (px // 4) * 128 : (px // 4) * 128 + 128]
            turn = ((iy - px % 4) * 32) % 128
            if turn:
                part = pltpu.roll(part, turn, 1)
            held = jnp.where(lane // 32 == iy, part, held)
        rows.append(held)
    waves_y = dot(jnp.concatenate(rows, axis=0), fwd_y[...])
    stacked = jnp.concatenate(
        [
            jnp.concatenate([waves_y[px * 48 + c * 16 : px * 48 + c * 16 + 16, :] for px in range(8)], axis=0)
            for c in range(3)
        ],
        axis=1,
    )
    full = dot(fwd_xz[...], stacked)
    inverse, slope_x = spectral[0:128, :], spectral[128:256, :]
    slope_y, slope_z = spectral[256:384, :], spectral[384:512, :]
    psi_real, psi_imag = [], []
    for c in range(3):
        low = full[:, c * 256 : c * 256 + 128]
        high = full[:, c * 256 + 128 : c * 256 + 256]
        psi_real.append((low[0:128] + high[128:256]) * inverse)
        psi_imag.append((high[0:128] - low[128:256]) * inverse)

    def cross(psi):
        return [
            slope_y * psi[2] - slope_z * psi[1],
            slope_z * psi[0] - slope_x * psi[2],
            slope_x * psi[1] - slope_y * psi[0],
        ]

    cross_real, cross_imag = cross(psi_real), cross(psi_imag)
    hats = jnp.concatenate([part for c in range(3) for part in (-cross_imag[c], cross_real[c])], axis=1)
    owners = (owner_ref[0], owner_ref[1])
    chosen = jnp.concatenate(
        [
            inv_xz[pl.ds(pl.multiple_of(side * 128 + (owner // 32) * 16, 16), 16), :]
            for side in range(2)
            for owner in owners
        ],
        axis=0,
    )
    near = dot(chosen, hats)
    lines = []
    for c in range(3):
        low = near[:, c * 256 : c * 256 + 128]
        high = near[:, c * 256 + 128 : c * 256 + 256]
        lines.append(jnp.concatenate([low[0:32] - high[32:64], high[0:32] + low[32:64]], axis=1))
    patches = dot(jnp.concatenate(lines, axis=0), inv_y[...])
    row96, lane96 = iota((96, 128), 0), iota((96, 128), 1)
    column = jnp.where((row96 // 16) % 2 == 0, owners[0] % 32, owners[1] % 32)
    patches = jnp.where(lane96 % 32 == column, patches, 0.0)
    turned = lax.dot_general(spread_y[...], patches, (((1,), (1,)), ((), ())), precision=HIGHEST,
                             preferred_element_type=jnp.float32)
    field[...] = dot(turned * match[...], spread_z[...])

    slot = slot_ref[0]
    on = [jnp.where(slot == b, 10.0, 0.0) for b in range(2)]

    def plane(x, carry):
        solid = mask_ref[pl.ds(pl.multiple_of(x * 8, 8), 8), :]
        for b in range(2):
            chi[pl.ds(x * 16 + b, 8, stride=2), :] = solid * on[b]
        for h in range(2):
            part = chi[pl.ds(pl.multiple_of(x * 16 + h * 8, 8), 8), :]
            scale = 1.0 / (1.0 + part)
            for c in range(3):
                lifted = field[pl.ds(pl.multiple_of((c * 4 + x // 8) * 16 + h * 8, 8), 8), :]
                there = u_ref[c * 32 + x, h * 8 : h * 8 + 8, :]
                out_ref[c * 32 + x, h * 8 : h * 8 + 8, :] = (there + lifted + part * speed_ref[0, c]) * scale
        return carry

    lax.fori_loop(0, 32, plane, 0)


VMEM = pl.BlockSpec(memory_space=pltpu.VMEM)
SMEM = pl.BlockSpec(memory_space=pltpu.SMEM)
LIMIT = 48 * 2**20


def f32(*shape):
    return jax.ShapeDtypeStruct(shape, jnp.float32)


def split(array):
    return array.reshape(2, 3, 256, 128).transpose(1, 2, 0, 3)


def join(array):
    return array.reshape(3, 256, 2, 128).transpose(2, 0, 1, 3).reshape(2, 3, 32768)


def body(vorticity, velocity, level_map, patch_owner, neighbours, fish_slot, fish_mask, fish_speed):
    w, u = split(vorticity), split(velocity)
    ghosts = pl.pallas_call(
        faces_kernel,
        out_shape=f32(576, 128),
        in_specs=[SMEM, VMEM, VMEM],
        out_specs=VMEM,
        scratch_shapes=[
            pltpu.VMEM((576, 128), jnp.float32),
            pltpu.VMEM((1152, 128), jnp.float32),
            pltpu.VMEM((576, 128), jnp.float32),
            pltpu.VMEM((576, 128), jnp.float32),
            pltpu.VMEM((192, 128), jnp.float32),
            pltpu.VMEM((8, 128), jnp.int32),
            pltpu.VMEM((64, 128), jnp.int32),
            pltpu.SemaphoreType.DMA((26,)),
            pltpu.SemaphoreType.DMA((26,)),
        ],
        compiler_params=pltpu.CompilerParams(collective_id=0, has_side_effects=True, vmem_limit_bytes=LIMIT),
        name="faces",
    )(neighbours, w.reshape(1536, 128), u.reshape(1536, 128))
    fold, pick, mean, spread_y, match, spread_z = (jnp.asarray(a) for a in fold_tables())
    fresh, tile = pl.pallas_call(
        stencil_kernel,
        out_shape=(f32(96, 16, 128), f32(8, 128)),
        in_specs=[SMEM, SMEM] + [VMEM] * 6,
        out_specs=(VMEM, VMEM),
        scratch_shapes=[
            pltpu.VMEM((192, 128), jnp.float32),
            pltpu.VMEM((1536, 128), jnp.float32),
            pltpu.VMEM((192, 128), jnp.float32),
            pltpu.VMEM((192, 128), jnp.float32),
        ],
        compiler_params=pltpu.CompilerParams(vmem_limit_bytes=LIMIT),
        name="stencil",
    )(level_map, patch_owner, w.reshape(96, 16, 128), u.reshape(96, 16, 128), ghosts, fold, pick, mean)
    gathered = pl.pallas_call(
        gather_kernel,
        out_shape=f32(256, 512),
        in_specs=[VMEM],
        out_specs=VMEM,
        scratch_shapes=[
            pltpu.VMEM((64, 128), jnp.float32),
            pltpu.VMEM((256, 512), jnp.float32),
            pltpu.SemaphoreType.DMA((17,)),
            pltpu.SemaphoreType.DMA((17,)),
        ],
        compiler_params=pltpu.CompilerParams(collective_id=1, has_side_effects=True, vmem_limit_bytes=LIMIT),
        name="gather",
    )(tile)
    tables = [jnp.asarray(a) for a in dft_tables()]
    moved = pl.pallas_call(
        solve_kernel,
        out_shape=f32(96, 16, 128),
        in_specs=[SMEM] * 3 + [VMEM] * 11,
        out_specs=VMEM,
        scratch_shapes=[pltpu.VMEM((512, 128), jnp.float32), pltpu.VMEM((192, 128), jnp.float32)],
        compiler_params=pltpu.CompilerParams(vmem_limit_bytes=LIMIT),
        name="solve",
    )(patch_owner, fish_slot, fish_speed, fish_mask.reshape(256, 128), u.reshape(96, 16, 128), gathered,
      *tables, spread_y, match, spread_z)
    return join(fresh), join(moved)


def solution(mesh):
    blocks = ("blk", "sub")
    placed = (
        P(blocks, None, None),
        P(blocks, None, None),
        P(blocks),
        P(blocks),
        P(blocks, None),
        P(blocks),
        P(blocks, None),
        P(blocks, None),
    )
    return jax.shard_map(
        body,
        mesh=mesh,
        in_specs=placed,
        out_specs=(P(blocks, None, None), P(blocks, None, None)),
        check_vma=False,
    )
```

time: 1050 us -> 65 us (0.06)
  the two profiles are of different devices: /device:TPU:1 before, /device:TPU:16 now
where the time goes in v1:
time: 65 us; the launch traced here: 64.8 us
  Pallas kernels  60.3 us (93%)
  local copies, waits for them, and re-layouts  3.01 us (5%)
  between operations  1.49 us (2%)
    pallas_call x1, Pallas kernels, body(): pl.pallas_call(faces_kernel, out_shape=f32(576, 128), in_specs=[SMEM, VME...  25.2 us
    pallas_call x1, Pallas kernels, body(): pl.pallas_call(gather_kernel, out_shape=f32(256, 512), in_specs=[VMEM], o...  22.4 us
    pallas_call x1, Pallas kernels, body(): pl.pallas_call(stencil_kernel, out_shape=(f32(96, 16, 128), f32(8, 128)),...  6.81 us
    pallas_call x1, Pallas kernels, body(): pl.pallas_call(solve_kernel, out_shape=f32(96, 16, 128), in_specs=[SMEM]...  5.88 us
    unnamed x36, local copies, waits for them, and re-layouts  3.01 us

profile of v1, /device:TPU:16, one launch (start us, length us, event | category | flops | bytes accessed | tf_op | source)
XLA Modules:
  0.0 64.8 jit_solution(743341979291991488)
XLA Ops:
  1.3 0.0 copy-start.15
  1.3 0.7 %copy-done.15 = s32[2,6]{1,0:T(2,128)S(1)} copy-done((s32[2,6]{1,0:T(2,128)S(1)}, s32[2,6]{1,0:T(2,128)}, u32[]{:S(2)}) %copy-start.15) | copy-done | bytes 72
  2.0 0.0 copy-start
  2.0 1.1 %copy-done = f32[2,3,32768]{2,0,1:T(2,128)S(1)} copy-done((f32[2,3,32768]{2,0,1:T(2,128)S(1)}, f32[2,3,32768]{2,0,1:T(2,128)}, u32[]{:S(2)}) %copy-start) | copy-done | bytes 786456
  3.1 0.0 copy-start.2
  3.1 1.1 %copy-done.2 = f32[2,3,32768]{2,0,1:T(2,128)S(1)} copy-done((f32[2,3,32768]{2,0,1:T(2,128)S(1)}, f32[2,3,32768]{2,0,1:T(2,128)}, u32[]{:S(2)}) %copy-start.2) | copy-done | bytes 786456
  4.2 0.0 copy-start.1
  4.2 0.0 copy-start.5
  4.2 0.0 copy-start.9
  4.2 0.0 copy-start.13
  4.2 0.0 copy-start.14
  4.2 0.0 copy-start.17
  4.3 25.2 %faces.1.gh_ref = f32[576,128]{1,0:T(8,128)S(1)} custom-call(s32[2,6]{1,0:T(2,128)S(1)} %copy-done.15, f32[1536,128]{1,0:T(8,128)S(1)} %bitcast.28, f32[1536,128]{1,0:T(8,128)S(1)} %bitcast.25), custom_call_target="tpu_custom_call" | custom-call | tf_op jit(solution)/shard_map/faces/pallas_call | solution.py:463
  29.4 0.0 copy-done.1
  29.5 0.0 copy-done.5
  29.5 0.0 copy-done.9
  29.5 0.0 copy-done.13
  29.5 0.0 copy-done.14
  29.5 0.0 copy-done.17
  29.5 0.0 copy-start.7
  29.5 0.0 copy-start.8
  29.5 0.0 copy-start.10
  29.5 0.0 copy-start.11
  29.6 0.0 copy-start.12
  29.6 6.8 %stencil.1 = (f32[96,16,128]{2,1,0:T(8,128)}, f32[8,128]{1,0:T(8,128)S(1)}) custom-call(s32[2]{0:T(128)S(1)} %copy-done.17, s32[2]{0:T(128)S(1)} %copy-done.14, f32[96,16,128]{2,1,0:T(8,128)S(1)} %bitcast.29, f32[96,16,128]{2,1,0:T(8,128)S(1)} %bitcast.26, f32[576,128]{1,0:T(8,128)S(1)} %faces.1.gh_ref, f32[128,256]{1,0:T(8,128)S(1)} %copy-done.9, ...), custom_call_target="tpu_custom_call" | custom-call | tf_op jit(solution)/shard_map/stencil/pallas_call | solution.py:483
  36.4 0.0 copy-start.3
  36.4 0.0 copy-start.4
  36.4 0.0 copy-start.6
  36.4 0.0 copy-start.16
  36.4 22.4 %gather.1.g_ref = f32[256,512]{1,0:T(8,128)S(1)} custom-call(f32[8,128]{1,0:T(8,128)S(1)} %get-tuple-element.5.tile_ref), custom_call_target="tpu_custom_call" | custom-call | tf_op jit(solution)/shard_map/gather/pallas_call | solution.py:497
  58.9 0.0 copy-done.7
  58.9 0.0 copy-done.8
  58.9 0.0 copy-done.10
  58.9 0.0 copy-done.11
  58.9 0.0 copy-done.12
  58.9 0.0 copy-done.3
  58.9 0.0 copy-done.4
  58.9 0.0 copy-done.6
  58.9 0.0 copy-done.16
  58.9 5.9 %solve.1 = f32[96,16,128]{2,1,0:T(8,128)} custom-call(s32[2]{0:T(128)S(1)} %copy-done.14, s32[1]{0:T(128)S(6)} %copy.25.slot_ref, f32[1,3]{1,0:T(1,128)S(1)} %copy-done.16, f32[256,128]{1,0:T(8,128)S(1)} %bitcast.30, f32[96,16,128]{2,1,0:T(8,128)S(1)} %bitcast.27, f32[256,512]{1,0:T(8,128)S(1)} %gather.1.g_ref, f32[128,256]{1,0:T(8,128)S(1)} %copy-done.8, ...), custom_call_target="tpu_custom_call" | custom-call | tf_op jit(solution)/shard_map/solve/pallas_call | solution.py:512
Async XLA Ops:
  1.3 0.7 %copy-start.15 = (s32[2,6]{1,0:T(2,128)S(1)}, s32[2,6]{1,0:T(2,128)}, u32[]{:S(2)}) copy-start(s32[2,6]{1,0:T(2,128)} %nb_ref.1) | copy-start | bytes 148
  2.0 1.1 %copy-start = (f32[2,3,32768]{2,0,1:T(2,128)S(1)}, f32[2,3,32768]{2,0,1:T(2,128)}, u32[]{:S(2)}) copy-start(f32[2,3,32768]{2,0,1:T(2,128)} %param.20) | copy-start | bytes 2359300
  3.1 1.1 %copy-start.2 = (f32[2,3,32768]{2,0,1:T(2,128)S(1)}, f32[2,3,32768]{2,0,1:T(2,128)}, u32[]{:S(2)}) copy-start(f32[2,3,32768]{2,0,1:T(2,128)} %param.19) | copy-start | bytes 2359300
  4.2 25.2 %copy-start.1 = (f32[2,3,32768]{2,0,1:T(2,128)S(1)}, f32[2,3,32768]{2,0,1:T(2,128)}, u32[]{:S(2)}) copy-start(f32[2,3,32768]{2,0,1:T(2,128)} %param.20) | copy-start | bytes 2359300
  4.2 25.2 %copy-start.5 = (f32[192,256]{1,0:T(8,128)S(1)}, f32[192,256]{1,0:T(8,128)}, u32[]{:S(2)}) copy-start(f32[192,256]{1,0:T(8,128)} %constant.21.clone.pick_ref) | copy-start | bytes 589828
  4.2 25.2 %copy-start.9 = (f32[128,256]{1,0:T(8,128)S(1)}, f32[128,256]{1,0:T(8,128)}, u32[]{:S(2)}) copy-start(f32[128,256]{1,0:T(8,128)} %constant.20.clone.fold_ref) | copy-start | bytes 393220
  4.2 25.2 %copy-start.13 = (f32[8,192]{1,0:T(8,128)S(1)}, f32[8,192]{1,0:T(8,128)}, u32[]{:S(2)}) copy-start(f32[8,192]{1,0:T(8,128)} %constant.22.clone.mean_ref) | copy-start | bytes 18436
  4.2 25.3 %copy-start.14 = (s32[2]{0:T(128)S(1)}, s32[2]{0:T(128)}, u32[]{:S(2)}) copy-start(s32[2]{0:T(128)} %owner_ref.3) | copy-start | bytes 28
  4.2 25.3 %copy-start.17 = (s32[2]{0:T(128)S(1)}, s32[2]{0:T(128)}, u32[]{:S(2)}) copy-start(s32[2]{0:T(128)} %level_ref.1) | copy-start | bytes 28
  29.5 29.3 %copy-start.7 = (f32[256,128]{1,0:T(8,128)S(1)}, f32[256,128]{1,0:T(8,128)}, u32[]{:S(2)}) copy-start(f32[256,128]{1,0:T(8,128)} %constant.28.clone.inv_y) | copy-start | bytes 393220
  29.5 29.3 %copy-start.8 = (f32[128,256]{1,0:T(8,128)S(1)}, f32[128,256]{1,0:T(8,128)}, u32[]{:S(2)}) copy-start(f32[128,256]{1,0:T(8,128)} %constant.26.clone.fwd_y) | copy-start | bytes 393220
  29.5 29.3 %copy-start.10 = (f32[192,96]{1,0:T(8,128)S(1)}, f32[192,96]{1,0:T(8,128)}, u32[]{:S(2)}) copy-start(f32[192,96]{1,0:T(8,128)} %constant.24.clone.match) | copy-start | bytes 221188
  29.5 29.3 %copy-start.11 = (f32[192,128]{1,0:T(8,128)S(1)}, f32[192,128]{1,0:T(8,128)}, u32[]{:S(2)}) copy-start(f32[192,128]{1,0:T(8,128)} %constant.23.clone.spread_y) | copy-start | bytes 294916
  29.6 29.3 %copy-start.12 = (f32[96,128]{1,0:T(8,128)S(1)}, f32[96,128]{1,0:T(8,128)}, u32[]{:S(2)}) copy-start(f32[96,128]{1,0:T(8,128)} %constant.25.clone.spread_z) | copy-start | bytes 147460
  36.4 22.5 %copy-start.3 = (f32[256,128]{1,0:T(8,128)S(1)}, f32[256,128]{1,0:T(8,128)}, u32[]{:S(2)}) copy-start(f32[256,128]{1,0:T(8,128)} %constant.27.clone.fwd_xz.inv_xz) | copy-start | bytes 393220
  36.4 22.5 %copy-start.4 = (f32[512,128]{1,0:T(8,128)S(1)}, f32[512,128]{1,0:T(8,128)}, u32[]{:S(2)}) copy-start(f32[512,128]{1,0:T(8,128)} %constant.29.clone.spectral) | copy-start | bytes 786436
  36.4 22.5 %copy-start.6 = (f32[1,32768]{1,0:T(1,128)S(1)}, f32[1,32768]{1,0:T(1,128)}, u32[]{:S(2)}) copy-start(f32[1,32768]{1,0:T(1,128)} %param.25) | copy-start | bytes 393220
  36.4 22.5 %copy-start.16 = (f32[1,3]{1,0:T(1,128)S(1)}, f32[1,3]{1,0:T(1,128)}, u32[]{:S(2)}) copy-start(f32[1,3]{1,0:T(1,128)} %speed_ref.1) | copy-start | bytes 40

commit v2 on v1

v2 whole, which is shorter than its diff:
```python
import math

import jax
import jax.numpy as jnp
import ml_dtypes
import numpy as np
from jax import lax
from jax.experimental import pallas as pl
from jax.experimental.pallas import tpu as pltpu
from jax.sharding import PartitionSpec as P

MESH = pl.DeviceIdType.MESH
RINGS = 32
GX = 32
GY = 128
GZ = 4


def fold_tables():
    row = np.arange(192)
    lane = np.arange(128)
    n = np.arange(256)
    row_c_ix, row_iy, row_b = row // 16, (row % 16) // 4, row % 2
    lane_iz = (lane % 32) // 8
    live = n < 192
    fold = ((lane_iz[:, None] == n[None, :] % 4) & live[None, :]) * 1.0
    pick = ((n[None, :] // 4 == (row_iy * 12 + row_c_ix)[:, None]) & live[None, :]) * 1.0
    mean = (np.arange(8)[:, None] == row_b[None, :]) / 512.0
    return fold.astype(np.float32), pick.astype(np.float32), mean.astype(np.float32)


def iota(shape, dim):
    return lax.broadcasted_iota(jnp.int32, shape, dim)


def place():
    blk, sub = lax.axis_index("blk"), lax.axis_index("sub")
    return blk // 2, lax.rem(blk, 2), sub


def row_pair(first, second):
    return jnp.where((iota((8, 128), 0) & 1) == 0, first, second)


class Chunk:
    def __init__(self, first, count, s1, r1, s2, r2, sem):
        self.first, self.count = first, count
        self.s1, self.r1, self.s2, self.r2, self.sem = s1, r1, s2, r2, sem
        self.rows = 12 * count

    def at(self, b, f, c):
        return (b * self.count + f - self.first) * 6 + c

    def put(self, b, f, c, plane):
        self.s1[pl.ds(self.at(b, f, c), 8, stride=self.rows), :] = plane

    def own(self, b, f, c):
        return self.s1[pl.ds(self.at(b, f, c), 8, stride=self.rows), :]

    def ghost(self, b, f, c):
        return self.r2[pl.ds(self.at(b, f, c), 8, stride=self.rows), :]

    def piece(self, which, count=1):
        return pl.ds(pl.multiple_of(which * self.rows, 8), count * self.rows)


def front_kernel(nb_ref, level_ref, owner_ref, slot_ref, speed_ref, w_hbm, u_hbm, mask_hbm, fold_hbm, pick_hbm, mean_hbm,
                 fresh_hbm, base_hbm, scale_hbm, g_hbm,
                 wv, uv, solid, fold_ref, pick_ref, mean_ref, out_ref, basis, scales, s1a, r1a, s2a, r2a, s1b, r1b, s2b, r2b,
                 tmp, nbs, nbr, acc, t1, g, in_sem, out_sem, ssem, rsem):
    ring, half, sub = place()
    me = half * 4 + sub
    core = lax.rem(sub, 2)
    y, z = ring // 8, lax.rem(ring, 8)
    wanted_here = ((w_hbm, wv), (u_hbm, uv), (mask_hbm, solid), (fold_hbm, fold_ref), (pick_hbm, pick_ref), (mean_hbm, mean_ref))
    loads = [pltpu.make_async_copy(src, dst, in_sem.at[n]) for n, (src, dst) in enumerate(wanted_here)]
    for load in loads:
        load.start()

    def mate(k):
        other = lax.bitwise_xor(me, k)
        return (ring * 2 + other // 4, lax.rem(other, 4))

    def beside(step):
        return (lax.rem(ring + step + RINGS, RINGS) * 2 + half, sub)

    def along_z(k):
        return ((y * 8 + lax.rem(z + k, 8)) * 2 + half, sub)

    def along_y(k):
        return ((lax.rem(y + k, 4) * 8 + z) * 2 + half, sub)

    mates = [mate(k) for k in range(1, 8)]
    on_z = [along_z(k) for k in range(1, 8)]
    on_y = [along_y(k) for k in range(1, 4)]
    everyone = mates + [beside(1), beside(-1)] + on_z + on_y
    barrier = pltpu.get_barrier_semaphore()
    for device in everyone:
        pl.semaphore_signal(barrier, inc=1, device_id=device, device_id_type=MESH)

    lane = iota((8, 128), 1)
    row = iota((8, 128), 0)
    wants = jnp.zeros((8, 128), jnp.int32)
    for b in range(2):
        for f in range(6):
            wants = jnp.where(lane == b * 6 + f, nb_ref[b, f] + half * 8, wants)
    nbs[...] = wants
    nbr[pl.ds(pl.multiple_of(me * 8, 8), 8), :] = wants
    for load in loads[:2]:
        load.wait()

    flat = (wv.reshape(1536, 128), uv.reshape(1536, 128))

    def source(c):
        return flat[c // 3], (c % 3) * 512

    def remote(src, dst, sem, device):
        return pltpu.make_async_remote_copy(
            src_ref=src, dst_ref=dst, send_sem=ssem.at[sem], recv_sem=rsem.at[sem],
            device_id=device, device_id_type=MESH)

    def start(copies):
        for copy in copies:
            copy.start()
        return copies

    def finish(copies):
        for copy in copies:
            copy.wait()

    xy = Chunk(0, 4, s1a, r1a, s2a, r2a, 8)
    zz = Chunk(4, 2, s1b, r1b, s2b, r2b, 24)

    def scatter_faces(part):
        copies = start([
            remote(part.s1.at[part.piece(lax.bitwise_xor(me, k))], part.r1.at[part.piece(4 + me)], part.sem + k - 1, mate(k))
            for k in range(1, 8)
        ])
        part.r1[part.piece(4 + me), :] = part.s1[part.piece(me), :]
        return copies

    def forward_faces(part):
        return start([
            remote(part.r1.at[part.piece(8, 4)], part.r1.at[part.piece(0, 4)], part.sem + 7, beside(1)),
            remote(part.r1.at[part.piece(4, 4)], part.r1.at[part.piece(12, 4)], part.sem + 8, beside(-1)),
        ])

    def return_faces(part):
        copies = start([
            remote(part.s2.at[part.piece(lax.bitwise_xor(me, k))], part.r2.at[part.piece(me)], part.sem + 8 + k, mate(k))
            for k in range(1, 8)
        ])
        part.r2[part.piece(me), :] = part.s2[part.piece(me), :]
        return copies

    for c in range(6):
        ref, base = source(c)
        for b in range(2):
            for f, x in ((0, 0), (1, 31)):
                xy.put(b, f, c, ref[pl.ds(base + x * 16 + b, 8, stride=2), :])
            low = high = jnp.zeros((8, 128), jnp.float32)
            for n in range(4):
                first = ref[pl.ds(base + n * 128 + b, 8, stride=16), :]
                last = ref[pl.ds(base + n * 128 + 14 + b, 8, stride=16), :]
                if n:
                    first = pltpu.roll(first, 32 * n, 1)
                if n != 3:
                    last = pltpu.roll(last, (32 * n + 32) % 128, 1)
                here = lane // 32 == n
                low = jnp.where(here, first, low)
                high = jnp.where(here, last, high)
            xy.put(b, 2, c, low)
            xy.put(b, 3, c, high)

    pl.semaphore_wait(barrier, len(everyone))
    mine = pl.ds(pl.multiple_of(me * 8, 8), 8)
    sent_wants = start([remote(nbs, nbr.at[mine], k - 1, mate(k)) for k in range(1, 8)])
    sent_xy = scatter_faces(xy)

    def gather_z(x, held):
        at_low = (lane & 31) == x
        at_high = (lane & 31) == ((x + 31) & 31)
        fresh = []
        for c in range(6):
            ref, base = source(c)
            for h in range(2):
                plane = ref[pl.ds(pl.multiple_of(base + x * 16 + h * 8, 8), 8), :]
                turned = pltpu.roll(plane, x, 1)
                low, high = held[(c * 2 + h) * 2], held[(c * 2 + h) * 2 + 1]
                fresh += [jnp.where(at_low, turned, low), jnp.where(at_high, turned, high)]
        return tuple(fresh)

    zero = jnp.zeros((8, 128), jnp.float32)
    packed = lax.fori_loop(0, 32, gather_z, (zero,) * 24)
    for c in range(6):
        for which in range(2):
            for h in range(2):
                at = (c * 2 + which) * 16 + h * 8
                plane = packed[(c * 2 + h) * 2 + which]
                tmp[at : at + 8, :] = pltpu.roll(plane, 97, 1) if which else plane
    for c in range(6):
        for which in range(2):
            for b in range(2):
                zz.put(b, 4 + which, c, tmp[pl.ds((c * 2 + which) * 16 + b, 8, stride=2), :])
    sent_zz = scatter_faces(zz)

    def scale(level):
        return lax.shift_left(1, level).astype(jnp.float32)

    sizes = [scale(level_ref[b]) for b in range(2)]
    slopes_of = [0.05 * 0.5 * size for size in sizes]
    spread_of = [0.05 * 0.1 * (size * size) for size in sizes]
    slope = row_pair(*slopes_of)
    spread = row_pair(*spread_of)

    def around(x, c, h):
        ref = (wv, uv)[c // 3]
        at = (c % 3) * 32 + x
        rows = slice(h * 8, h * 8 + 8)
        here = ref[at, rows, :]
        left = jnp.zeros_like(here) if isinstance(x, int) and x == 0 else ref[at - 1, rows, :]
        right = jnp.zeros_like(here) if isinstance(x, int) and x == 31 else ref[at + 1, rows, :]
        if h == 0:
            before = jnp.where(row < 2, 0.0, pltpu.roll(here, 2, 0))
            after = ref[at, 2:10, :]
        else:
            before = ref[at, 6:14, :]
            after = jnp.where(row >= 6, 0.0, pltpu.roll(here, 6, 0))
        before = pltpu.roll(jnp.where(lane >= 96, before, here), 32, 1)
        after = pltpu.roll(jnp.where(lane < 32, after, here), 96, 1)
        below = jnp.where((lane & 31) == 0, 0.0, pltpu.roll(here, 1, 1))
        above = jnp.where((lane & 31) == 31, 0.0, pltpu.roll(here, 127, 1))
        return here, (left, right), (before, after), (below, above)

    def plane(x):
        for h in range(2):
            parts = [around(x, c, h) for c in range(6)]
            heres = [part[0] for part in parts]
            slopes = [[part[1 + d][1] - part[1 + d][0] for d in range(3)] for part in parts]
            for i in range(3):
                turn = heres[0] * slopes[3 + i][0] + heres[1] * slopes[3 + i][1] + heres[2] * slopes[3 + i][2]
                turn -= heres[3] * slopes[i][0] + heres[4] * slopes[i][1] + heres[5] * slopes[i][2]
                ends = [part for d in range(3) for part in parts[i][1 + d]]
                total = (ends[0] + ends[1]) + (ends[2] + ends[3]) + (ends[4] + ends[5])
                out_ref[i * 32 + x, h * 8 : h * 8 + 8, :] = (
                    heres[i] + slope * turn + spread * (total - 6.0 * heres[i])
                )

    def planes(low, high):
        def step(x, carry):
            plane(x)
            return carry

        lax.fori_loop(low, high, step, 0)

    plane(0)
    planes(1, 15)
    finish(sent_wants)
    finish(sent_xy)
    sent_xy = forward_faces(xy)
    planes(15, 23)
    finish(sent_zz)
    sent_zz = forward_faces(zz)
    planes(23, 31)
    plane(31)

    slot = iota((8, 32), 1)
    dead_low = (ring == 0).astype(jnp.int32)
    dead_high = (ring == RINGS - 1).astype(jnp.int32)
    alive = 1 - dead_low * (slot < 8).astype(jnp.int32) - dead_high * (slot >= 24).astype(jnp.int32)
    alive = alive.astype(jnp.float32)

    def select(part):
        wanted = nbr[pl.ds(0, 8, stride=8), :]
        for f in range(part.first, part.first + part.count):
            hot = jnp.concatenate(
                [jnp.where(wanted[:, b * 6 + f : b * 6 + f + 1] == slot, alive, 0.0) for b in range(2)], axis=0)
            data = jnp.concatenate(
                [part.r1[pl.ds(part.at(0, f ^ 1, c), 32, stride=6 * part.count), :] for c in range(6)], axis=1)
            hot = hot.astype(jnp.bfloat16)
            got = sum(dot(hot, third) for third in thirds(data))
            for b in range(2):
                for c in range(6):
                    part.s2[pl.ds(part.at(b, f, c), 8, stride=part.rows), :] = (
                        got[b * 8 : b * 8 + 8, c * 128 : c * 128 + 128]
                    )

    finish(sent_xy)
    select(xy)
    sent_xy = return_faces(xy)
    finish(sent_zz)
    select(zz)
    sent_zz = return_faces(zz)

    moved = out_ref.reshape(1536, 128)

    def added(part, b, f):
        ghosts = [part.ghost(b, f, c) for c in range(6)]
        vort, veloc = part.own(b, f, f // 2), part.own(b, f, 3 + f // 2)
        sign = slopes_of[b] * (1.0 if f % 2 else -1.0)
        vort, veloc = vort * sign, spread_of[b] - veloc * sign
        return [vort * ghosts[3 + i] + veloc * ghosts[i] for i in range(3)]

    finish(sent_xy)
    for b in range(2):
        for f, x in ((0, 0), (1, 31)):
            for i, extra in enumerate(added(xy, b, f)):
                moved[pl.ds(i * 512 + x * 16 + b, 8, stride=2), :] += extra
        for f, at, zone in ((2, 0, 0), (3, 14, 3)):
            for i, extra in enumerate(added(xy, b, f)):
                for n in range(4):
                    turn = (32 * (zone - n)) % 128
                    part = pltpu.roll(extra, turn, 1) if turn else extra
                    moved[pl.ds(i * 512 + n * 128 + at + b, 8, stride=16), :] += jnp.where(lane // 32 == zone, part, 0.0)
    finish(sent_zz)
    for b in range(2):
        for which in range(2):
            for i, extra in enumerate(added(zz, b, 4 + which)):
                tmp[pl.ds((i * 2 + which) * 16 + b, 8, stride=2), :] = extra
    ends = [[tmp[n * 16 + h * 8 : n * 16 + h * 8 + 8, :] for h in range(2)] for n in range(6)]

    def close(ix, carry):
        sums = [jnp.zeros((8, 128), jnp.float32)] * 6
        for step in range(8):
            x = ix * 8 + step
            for i in range(3):
                for h in range(2):
                    low = pltpu.roll(ends[i * 2][h], (128 - x) & 127, 1)
                    high = pltpu.roll(ends[i * 2 + 1][h], (159 - x) & 127, 1)
                    extra = jnp.where((lane & 31) == 0, low, jnp.where((lane & 31) == 31, high, 0.0))
                    fresh = out_ref[i * 32 + x, h * 8 : h * 8 + 8, :] + extra
                    out_ref[i * 32 + x, h * 8 : h * 8 + 8, :] = fresh
                    sums[i * 2 + h] = sums[i * 2 + h] + fresh
        for i in range(3):
            for h in range(2):
                acc[pl.ds(pl.multiple_of((i * 4 + ix) * 16 + h * 8, 8), 8), :] = sums[i * 2 + h]
        return carry

    lax.fori_loop(0, 4, close, 0)

    stores = [pltpu.make_async_copy(out_ref, fresh_hbm, out_sem.at[0])]
    stores[0].start()
    for load in loads[2:]:
        load.wait()
    fold, mean = fold_ref[...].astype(jnp.bfloat16), mean_ref[...].astype(jnp.bfloat16)
    folded = sum(dot(part, fold) for part in thirds(acc[...])) * pick_ref[...]
    rows = sum(dot(mean, part) for part in thirds(folded))
    wide_row, wide_lane = iota((8, 256), 0), iota((8, 256), 1)

    def shrink(level):
        return jnp.where(level == 0, 1.0, jnp.where(level == 1, 0.125, 0.015625))

    rows = rows * jnp.where(wide_row == 0, shrink(level_ref[0]), shrink(level_ref[1]))
    owners = jnp.where(wide_row == 0, owner_ref[0], owner_ref[1]).astype(jnp.float32)
    rows = jnp.where(wide_lane == 192, owners, rows)
    gap = jnp.zeros((2, 128), jnp.float32)
    spot = half * 2 + sub // 2
    mine = pl.ds(pl.multiple_of(spot * 8, 8), 8)
    t1[mine, :] = jnp.concatenate(
        [rows[0:1, 0:128], rows[0:1, 128:256], gap, rows[1:2, 0:128], rows[1:2, 128:256], gap], axis=0)

    def share(ref, targets, first):
        return start([remote(ref, ref, first + n, device) for n, device in enumerate(targets)])

    sent = share(t1.at[mine], [mates[k - 1] for k in (2, 4, 6)], 40)

    on = [jnp.where(slot_ref[0] == b, 10.0, 0.0) for b in range(2)]
    flat_scale = scales.reshape(512, 128)

    def penalise(x, carry):
        part = solid[pl.ds(pl.multiple_of(x * 8, 8), 8), :]
        for b in range(2):
            flat_scale[pl.ds(x * 16 + b, 8, stride=2), :] = part * on[b]
        for h in range(2):
            rows = slice(h * 8, h * 8 + 8)
            chi = scales[x, rows, :]
            scale = 1.0 / (1.0 + chi)
            scales[x, rows, :] = scale
            for c in range(3):
                basis[c * 32 + x, rows, :] = (uv[c * 32 + x, rows, :] + chi * speed_ref[0, c]) * scale
        return carry

    lax.fori_loop(0, 32, penalise, 0)
    stores += start([
        pltpu.make_async_copy(basis, base_hbm, out_sem.at[1]),
        pltpu.make_async_copy(scales, scale_hbm, out_sem.at[2]),
    ])
    finish(sent)
    first = core * 256
    at = pl.ds(pl.multiple_of(first + ring * 8, 8), 8)
    for t in range(2):
        g[at, t * 128 : t * 128 + 128] = t1[pl.ds(t, 8, stride=4), :]
    finish(share(g.at[at], on_z, 43))
    finish(share(g.at[pl.ds(pl.multiple_of(first + y * 64, 64), 64)], on_y, 50))
    own_half = pl.ds(pl.multiple_of(first, 256), 256)
    other_half = pl.ds(pl.multiple_of(256 - first, 256), 256)
    sent = share(g.at[own_half], [mates[0]], 53)
    stores += start([pltpu.make_async_copy(g.at[own_half], g_hbm.at[own_half], out_sem.at[3])])
    finish(sent)
    stores += start([pltpu.make_async_copy(g.at[other_half], g_hbm.at[other_half], out_sem.at[4])])
    finish(stores)


def halves(table):
    high = table.astype(ml_dtypes.bfloat16).astype(np.float64)
    low = (table - high).astype(ml_dtypes.bfloat16).astype(np.float64)
    return high, low


def solve_tables():
    space = np.arange(128)
    px, ix, iz = space // 16, (space // 4) % 4, space % 4
    x, z = 4 * px + ix, iz
    kx, kz = space // 4, space % 4
    iy, py = space // 32, space % 32
    y = 4 * py + iy
    ky = space
    theta = 2.0 * np.pi * ((kx[:, None] * x[None, :] % 32) / 32.0 + (kz[:, None] * z[None, :] % 4) / 4.0)
    phi = 2.0 * np.pi * ((y[:, None] * ky[None, :]) % 128) / 128.0
    high, low = halves(np.concatenate([np.cos(phi), -np.sin(phi)], axis=1))
    fwd_y = np.concatenate([high, high, low], axis=0)
    high, low = halves(np.concatenate([np.cos(theta), np.sin(theta)], axis=0))
    fwd_xz = np.concatenate([high, low], axis=1)
    inv_xz = np.concatenate([np.cos(theta.T), np.sin(theta.T)], axis=0).astype(np.float32)
    line = np.arange(256)
    turn = 2.0 * np.pi * (((4 * (line // 8) + (line % 8) // 2)[:, None] * ky[None, :]) % 128) / 128.0
    inv_y = (np.concatenate([np.cos(turn), -np.sin(turn)], axis=1) / 16384.0).astype(np.float32)

    def waves(index, length):
        signed = np.where(index < (length + 1) // 2, index, index - length)
        full = signed * (2.0 * math.pi / length)
        return full, np.where(index == length // 2, 0.0, full)

    full_x, slope_x = waves(kx, GX)
    full_y, slope_y = waves(ky, GY)
    full_z, slope_z = waves(kz, GZ)
    square = (full_x**2 + full_z**2)[:, None] + (full_y**2)[None, :]
    inverse = np.where(square > 0, 1.0 / np.where(square > 0, square, 1.0), 0.0)
    spectral = np.concatenate([inverse * slope_x[:, None], inverse * slope_y[None, :], inverse * slope_z[:, None]])
    src = np.arange(96)
    row = np.arange(192)
    src_c, src_b, src_ix, src_iz = src // 32, (src // 16) % 2, (src // 4) % 4, src % 4
    match = ((src_c * 4 + src_ix)[None, :] == (row // 16)[:, None]) & (src_b[None, :] == (row % 2)[:, None])
    spread_z = src_iz[:, None] == ((np.arange(128) % 32) // 8)[None, :]
    return tuple(a.astype(np.float32) for a in (inv_xz, inv_y, fwd_y, fwd_xz, spectral, match * 1.0, spread_z * 1.0))


def cut(array):
    high = array.astype(jnp.bfloat16)
    return high, (array - high.astype(jnp.float32)).astype(jnp.bfloat16)


def thirds(array):
    high = array.astype(jnp.bfloat16)
    rest = array - high.astype(jnp.float32)
    middle = rest.astype(jnp.bfloat16)
    return high, middle, (rest - middle.astype(jnp.float32)).astype(jnp.bfloat16)


def dot(left, right):
    return jnp.dot(left, right, preferred_element_type=jnp.float32)


def dot_nt(left, right):
    return lax.dot_general(left, right, (((1,), (1,)), ((), ())), preferred_element_type=jnp.float32)


def solve(owners, ready, g_ref, inv_xz, inv_y, fwd_y, fwd_xz, spectral, match, spread_z, near_y):
    ready(0)
    sent = g_ref[...]
    hot = (sent[:, 192:193] == iota((512, 256), 1).astype(jnp.float32)).astype(jnp.bfloat16)
    high, low = cut(sent.T)
    columns = dot(high, hot) + dot(low, hot)
    ready(1)
    ready(2)
    for b in range(2):
        rows = pl.ds(pl.multiple_of((owners[b] % 32) * 8, 8), 8)
        for n in range(2):
            near_y[pl.ds(n * 16 + b, 8, stride=2), :] = inv_y[rows, n * 128 : n * 128 + 128]
    near_high, near_low = cut(jnp.concatenate([near_y[0:16, :], near_y[16:32, :]], axis=1))
    chosen_high, chosen_low = cut(jnp.concatenate(
        [
            inv_xz[pl.ds(pl.multiple_of(side * 128 + (owner // 32) * 16, 16), 16), :]
            for side in range(2)
            for owner in owners
        ],
        axis=0,
    ))
    lane = iota((48, 128), 1)
    rows = []
    for px in range(8):
        held = None
        for iy in range(4):
            part = columns[iy * 48 : iy * 48 + 48, (px // 4) * 128 : (px // 4) * 128 + 128]
            turn = ((iy - px % 4) * 32) % 128
            if turn:
                part = pltpu.roll(part, turn, 1)
            held = part if held is None else jnp.where(lane >= iy * 32, part, held)
        rows.append(held)
    high, low = cut(jnp.concatenate(rows, axis=0))
    ready(3)
    table = fwd_y[...].astype(jnp.bfloat16)
    waves_y = dot(jnp.concatenate([high, low], axis=1), table[0:256]) + dot(high, table[256:384])
    stacked = jnp.concatenate(
        [
            jnp.concatenate([waves_y[px * 48 + c * 16 : px * 48 + c * 16 + 16, :] for px in range(8)], axis=0)
            for c in range(3)
        ],
        axis=1,
    )
    high, low = cut(stacked)
    ready(4)
    table = fwd_xz[...].astype(jnp.bfloat16)
    full = dot(table, jnp.concatenate([high, high], axis=0)) + dot(table[:, 0:128], low)
    for n in range(5, 8):
        ready(n)
    slope_x, slope_y, slope_z = spectral[0:128, :], spectral[128:256, :], spectral[256:384, :]
    real, imag = [], []
    for c in range(3):
        low = full[:, c * 256 : c * 256 + 128]
        high = full[:, c * 256 + 128 : c * 256 + 256]
        real.append(low[0:128] + high[128:256])
        imag.append(high[0:128] - low[128:256])

    def cross(hat):
        return [
            slope_y * hat[2] - slope_z * hat[1],
            slope_z * hat[0] - slope_x * hat[2],
            slope_x * hat[1] - slope_y * hat[0],
        ]

    cross_real, cross_imag = cross(real), cross(imag)
    high, low = cut(jnp.concatenate([part for c in range(3) for part in (-cross_imag[c], cross_real[c])], axis=1))
    near = dot(jnp.concatenate([chosen_high, chosen_low], axis=1), jnp.concatenate([high, high], axis=0))
    near = near + dot(chosen_high, low)
    lines = []
    for c in range(3):
        low = near[:, c * 256 : c * 256 + 128]
        high = near[:, c * 256 + 128 : c * 256 + 256]
        lines.append(jnp.concatenate([low[0:32] - high[32:64], high[0:32] + low[32:64]], axis=1))
    high, low = cut(jnp.concatenate(lines, axis=0))
    turned = dot_nt(near_high, high) + (dot_nt(near_high, low) + dot_nt(near_low, high))
    high, low = cut(jnp.concatenate([turned] * 12, axis=0) * match[...])
    table = spread_z[...].astype(jnp.bfloat16)
    return dot(high, table) + dot(low, table)


def solve_kernel(owner_ref, *refs):
    sources, (fresh_out, out_hbm), refs = refs[:11], refs[11:13], refs[13:]
    held, (near_y, field, moved, sem, out_sem) = refs[:11], refs[11:]
    loads = [pltpu.make_async_copy(src, dst, sem.at[n]) for n, (src, dst) in enumerate(zip(sources, held))]
    for load in loads:
        load.start()
    base, scale, fresh = held[8:]
    owners = (owner_ref[0], owner_ref[1])
    stores = [pltpu.make_async_copy(fresh, fresh_out, out_sem.at[12])]

    def ready(n):
        loads[n].wait()
        if n == 7:
            loads[10].wait()
            stores[0].start()

    field[...] = solve(owners, ready, *held[:8], near_y)
    for load in loads[8:10]:
        load.wait()
    for ix in range(4):
        lifted = [[field[(c * 4 + ix) * 16 + h * 8 : (c * 4 + ix) * 16 + h * 8 + 8, :] for h in range(2)] for c in range(3)]
        for x in range(ix * 8, ix * 8 + 8):
            for h in range(2):
                rows = slice(h * 8, h * 8 + 8)
                part = scale[x, rows, :]
                for c in range(3):
                    moved[c * 32 + x, rows, :] = base[c * 32 + x, rows, :] + lifted[c][h] * part
        for c in range(3):
            planes = pl.ds(c * 32 + ix * 8, 8)
            stores.append(pltpu.make_async_copy(moved.at[planes], out_hbm.at[planes], out_sem.at[ix * 3 + c]))
            stores[-1].start()
    for copy in stores:
        copy.wait()


VMEM = pl.BlockSpec(memory_space=pltpu.VMEM)
SMEM = pl.BlockSpec(memory_space=pltpu.SMEM)
ANY = pl.BlockSpec(memory_space=pl.ANY)
LIMIT = 62 * 2**20


def f32(*shape):
    return jax.ShapeDtypeStruct(shape, jnp.float32)


def scratch(*shape):
    return pltpu.VMEM(shape, jnp.float32)


def split(array):
    return array.reshape(2, 3, 256, 128).transpose(1, 2, 0, 3)


def join(array):
    return array.reshape(3, 256, 2, 128).transpose(2, 0, 1, 3).reshape(2, 3, 32768)


def body(vorticity, velocity, level_map, patch_owner, neighbours, fish_slot, fish_mask, fish_speed):
    w, u = split(vorticity), split(velocity)
    w, u = w.reshape(96, 16, 128), u.reshape(96, 16, 128)
    field = f32(96, 16, 128)

    def faces(count):
        return [scratch(rows * count, 128) for rows in (96, 192, 96, 96)]

    fresh, base, scale, gathered = pl.pallas_call(
        front_kernel,
        out_shape=(field, field, f32(32, 16, 128), f32(512, 256)),
        in_specs=[SMEM] * 5 + [ANY] * 6,
        out_specs=(ANY,) * 4,
        scratch_shapes=[
            scratch(96, 16, 128),
            scratch(96, 16, 128),
            scratch(256, 128),
            scratch(128, 256),
            scratch(192, 256),
            scratch(8, 192),
            scratch(96, 16, 128),
            scratch(96, 16, 128),
            scratch(32, 16, 128),
            *faces(4),
            *faces(2),
            scratch(192, 128),
            pltpu.VMEM((8, 128), jnp.int32),
            pltpu.VMEM((64, 128), jnp.int32),
            scratch(192, 128),
            scratch(32, 128),
            scratch(512, 256),
            pltpu.SemaphoreType.DMA((6,)),
            pltpu.SemaphoreType.DMA((5,)),
            pltpu.SemaphoreType.DMA((56,)),
            pltpu.SemaphoreType.DMA((56,)),
        ],
        compiler_params=pltpu.CompilerParams(collective_id=0, has_side_effects=True, vmem_limit_bytes=LIMIT),
        name="front",
    )(neighbours, level_map, patch_owner, fish_slot, fish_speed, w, u, fish_mask.reshape(256, 128),
      *(jnp.asarray(a) for a in fold_tables()))
    sources = (gathered, *(jnp.asarray(a) for a in solve_tables()), base, scale, fresh)
    fresh, moved = pl.pallas_call(
        solve_kernel,
        out_shape=(field, field),
        in_specs=[SMEM] + [ANY] * 11,
        out_specs=(ANY, ANY),
        scratch_shapes=[
            *(scratch(*array.shape) for array in sources),
            scratch(32, 128),
            scratch(192, 128),
            scratch(96, 16, 128),
            pltpu.SemaphoreType.DMA((11,)),
            pltpu.SemaphoreType.DMA((13,)),
        ],
        compiler_params=pltpu.CompilerParams(vmem_limit_bytes=LIMIT),
        name="solve",
    )(patch_owner, *sources)
    return join(fresh), join(moved)


def solution(mesh):
    blocks = ("blk", "sub")
    placed = (
        P(blocks, None, None),
        P(blocks, None, None),
        P(blocks),
        P(blocks),
        P(blocks, None),
        P(blocks),
        P(blocks, None),
        P(blocks, None),
    )
    return jax.shard_map(
        body,
        mesh=mesh,
        in_specs=placed,
        out_specs=(P(blocks, None, None), P(blocks, None, None)),
        check_vma=False,
    )
```

time: 65 us -> 50.1 us (0.77)
  the two profiles are of different devices: /device:TPU:16 before, /device:TPU:1 now
where the time goes in v2:
time: 50.1 us; the launch traced here: 50 us
  Pallas kernels  48.7 us (97%)
  between operations  1.29 us (3%)
    pallas_call x1, Pallas kernels, body(): pl.pallas_call(front_kernel, out_shape=(field, field, f32(32, 16, 128), f...  43.7 us
    pallas_call x1, Pallas kernels, body(): pl.pallas_call(solve_kernel, out_shape=(field, field), in_specs=[SMEM] +...  5.04 us

profile of v2, /device:TPU:1, one launch (start us, length us, event | category | flops | bytes accessed | tf_op | source)
XLA Modules:
  0.0 50.0 jit_solution(5517594828136703337)
XLA Ops:
  1.3 43.7 %front.1 = (f32[96,16,128]{2,1,0:T(8,128)}, f32[96,16,128]{2,1,0:T(8,128)}, f32[32,16,128]{2,1,0:T(8,128)}, f32[512,256]{1,0:T(8,128)}) custom-call(s32[2,6]{1,0:T(2,128)} %nb_ref.1, s32[2]{0:T(128)} %level_ref.1, s32[2]{0:T(128)} %owner_ref.3, s32[1]{0:T(128)S(6)} %copy.24.slot_ref, f32[1,3]{1,0:T(1,128)} %speed_ref.1, f32[96,16,128]{2,1,0:T(8,128)} %bitcast.21, ...), custom_call_target="tpu_custom_call" | custom-call | tf_op jit(solution)/shard_map/front/pallas_call | solution.py:613
  44.9 5.0 %solve.1 = (f32[96,16,128]{2,1,0:T(8,128)}, f32[96,16,128]{2,1,0:T(8,128)}) custom-call(s32[2]{0:T(128)} %owner_ref.3, f32[512,256]{1,0:T(8,128)} %get-tuple-element.8.refs_0_, f32[256,128]{1,0:T(8,128)} %constant.23.clone.refs_1_, f32[256,256]{1,0:T(8,128)} %constant.24.clone.refs_2_, f32[384,256]{1,0:T(8,128)} %constant.25.clone.refs_3_, ...), custom_call_target="tpu_custom_call" | custom-call | tf_op jit(solution)/shard_map/solve/pallas_call | solution.py:646

commit v3 on v2

--- a/solution.py
+++ b/solution.py
@@ -64,16 +64,17 @@
         return pl.ds(pl.multiple_of(which * self.rows, 8), count * self.rows)
 
 
-def front_kernel(nb_ref, level_ref, owner_ref, slot_ref, speed_ref, w_hbm, u_hbm, mask_hbm, fold_hbm, pick_hbm, mean_hbm,
-                 fresh_hbm, base_hbm, scale_hbm, g_hbm,
-                 wv, uv, solid, fold_ref, pick_ref, mean_ref, out_ref, basis, scales, s1a, r1a, s2a, r2a, s1b, r1b, s2b, r2b,
-                 tmp, nbs, nbr, acc, t1, g, in_sem, out_sem, ssem, rsem):
+def front_kernel(nb_ref, level_ref, owner_ref, speed_ref, slot_hbm, *refs):
+    sources, (fresh_hbm, both_hbm, field_hbm), refs = refs[:13], refs[13:16], refs[16:]
+    held, refs = refs[:13], refs[13:]
+    wv, uv, solid, fold_ref, pick_ref, mean_ref, inv_xz, inv_y, fwd_y, fwd_xz, spectral, match, spread_z = held
+    (out_ref, both, field, s1a, r1a, s2a, r2a, s1b, r1b, s2b, r2b, tmp, nbs, nbr, acc, t1, g, chosen, near_y, mine_s, peer_s,
+     slot_ref, in_sem, out_sem, ssem, rsem) = refs
     ring, half, sub = place()
     me = half * 4 + sub
-    core = lax.rem(sub, 2)
     y, z = ring // 8, lax.rem(ring, 8)
-    wanted_here = ((w_hbm, wv), (u_hbm, uv), (mask_hbm, solid), (fold_hbm, fold_ref), (pick_hbm, pick_ref), (mean_hbm, mean_ref))
-    loads = [pltpu.make_async_copy(src, dst, in_sem.at[n]) for n, (src, dst) in enumerate(wanted_here)]
+    loads = [pltpu.make_async_copy(src, dst, in_sem.at[n]) for n, (src, dst) in enumerate(zip(sources, held))]
+    loads.append(pltpu.make_async_copy(slot_hbm, slot_ref, in_sem.at[13]))
     for load in loads:
         load.start()
 
@@ -104,6 +105,7 @@
     for b in range(2):
         for f in range(6):
             wants = jnp.where(lane == b * 6 + f, nb_ref[b, f] + half * 8, wants)
+        wants = jnp.where(lane == 12 + b, owner_ref[b], wants)
     nbs[...] = wants
     nbr[pl.ds(pl.multiple_of(me * 8, 8), 8), :] = wants
     for load in loads[:2]:
@@ -365,39 +367,67 @@
     sent = share(t1.at[mine], [mates[k - 1] for k in (2, 4, 6)], 40)
 
     on = [jnp.where(slot_ref[0] == b, 10.0, 0.0) for b in range(2)]
-    flat_scale = scales.reshape(512, 128)
+    flat_both = both.reshape(2048, 128)
 
     def penalise(x, carry):
         part = solid[pl.ds(pl.multiple_of(x * 8, 8), 8), :]
+        at = (x // 16) * 64 + lax.rem(x, 16)
         for b in range(2):
-            flat_scale[pl.ds(x * 16 + b, 8, stride=2), :] = part * on[b]
+            flat_both[pl.ds((at + 48) * 16 + b, 8, stride=2), :] = part * on[b]
         for h in range(2):
             rows = slice(h * 8, h * 8 + 8)
-            chi = scales[x, rows, :]
+            chi = both[at + 48, rows, :]
             scale = 1.0 / (1.0 + chi)
-            scales[x, rows, :] = scale
+            both[at + 48, rows, :] = scale
             for c in range(3):
-                basis[c * 32 + x, rows, :] = (uv[c * 32 + x, rows, :] + chi * speed_ref[0, c]) * scale
+                both[at + c * 16, rows, :] = (uv[c * 32 + x, rows, :] + chi * speed_ref[0, c]) * scale
         return carry
 
     lax.fori_loop(0, 32, penalise, 0)
-    stores += start([
-        pltpu.make_async_copy(basis, base_hbm, out_sem.at[1]),
-        pltpu.make_async_copy(scales, scale_hbm, out_sem.at[2]),
-    ])
+    stores += start([pltpu.make_async_copy(both, both_hbm, out_sem.at[1])])
     finish(sent)
-    first = core * 256
-    at = pl.ds(pl.multiple_of(first + ring * 8, 8), 8)
+    first = ring * 8
+    at = pl.ds(pl.multiple_of(first, 8), 8)
     for t in range(2):
         g[at, t * 128 : t * 128 + 128] = t1[pl.ds(t, 8, stride=4), :]
-    finish(share(g.at[at], on_z, 43))
-    finish(share(g.at[pl.ds(pl.multiple_of(first + y * 64, 64), 64)], on_y, 50))
-    own_half = pl.ds(pl.multiple_of(first, 256), 256)
-    other_half = pl.ds(pl.multiple_of(256 - first, 256), 256)
-    sent = share(g.at[own_half], [mates[0]], 53)
-    stores += start([pltpu.make_async_copy(g.at[own_half], g_hbm.at[own_half], out_sem.at[3])])
+    sent = share(g.at[at], on_z, 43)
+
+    theirs = nbr[pl.ds(pl.multiple_of(lax.bitwise_xor(me, 1) * 8, 8), 8), :]
+    owners = [jnp.full((8, 128), owner_ref[b], jnp.int32) for b in range(2)]
+    owners += [jnp.broadcast_to(theirs[:, 12 + b : 13 + b], (8, 128)) for b in range(2)]
+    columns = [owner & 31 for owner in owners]
+    bands = [owner // 32 for owner in owners]
+
+    def pick_y(py, carry):
+        found = []
+        for n in range(2):
+            row_of = inv_y[pl.ds(pl.multiple_of(py * 8, 8), 8), n * 128 : n * 128 + 128]
+            found += [jnp.where(columns[k] == py, row_of, carry[n * 4 + k]) for k in range(4)]
+        return tuple(found)
+
+    for n, part in enumerate(lax.fori_loop(0, 32, pick_y, (zero,) * 8)):
+        near_y[pl.ds((n % 4 // 2) * 32 + (n // 4) * 16 + n % 2, 8, stride=2), :] = part
+
+    def pick_xz(px, carry):
+        found = []
+        for n in range(4):
+            row_of = inv_xz[pl.ds(pl.multiple_of((n // 2) * 128 + px * 16 + (n % 2) * 8, 8), 8), :]
+            found += [jnp.where(bands[k] == px, row_of, carry[n * 4 + k]) for k in range(4)]
+        return tuple(found)
+
+    for n, part in enumerate(lax.fori_loop(0, 8, pick_xz, (zero,) * 16)):
+        k, n = n % 4, n // 4
+        to = (k // 2) * 64 + (n // 2) * 32 + (k % 2) * 16 + (n % 2) * 8
+        chosen[to : to + 8, :] = part
     finish(sent)
-    stores += start([pltpu.make_async_copy(g.at[other_half], g_hbm.at[other_half], out_sem.at[4])])
+    finish(share(g.at[pl.ds(pl.multiple_of(y * 64, 64), 64)], on_y, 50))
+
+    own, other = solve(g[...], fwd_y, fwd_xz, spectral, chosen, near_y)
+    mine_s[:, 0:96] = other
+    sent = start([remote(mine_s, peer_s, 53, mates[0])])
+    finish(sent)
+    field[...] = lift(own + peer_s[:, 0:96], match, spread_z)
+    stores += start([pltpu.make_async_copy(field, field_hbm, out_sem.at[2])])
     finish(stores)
 
 
@@ -465,27 +495,10 @@
     return lax.dot_general(left, right, (((1,), (1,)), ((), ())), preferred_element_type=jnp.float32)
 
 
-def solve(owners, ready, g_ref, inv_xz, inv_y, fwd_y, fwd_xz, spectral, match, spread_z, near_y):
-    ready(0)
-    sent = g_ref[...]
-    hot = (sent[:, 192:193] == iota((512, 256), 1).astype(jnp.float32)).astype(jnp.bfloat16)
+def solve(sent, fwd_y, fwd_xz, spectral, chosen, near_y):
+    hot = (sent[:, 192:193] == iota((256, 256), 1).astype(jnp.float32)).astype(jnp.bfloat16)
     high, low = cut(sent.T)
     columns = dot(high, hot) + dot(low, hot)
-    ready(1)
-    ready(2)
-    for b in range(2):
-        rows = pl.ds(pl.multiple_of((owners[b] % 32) * 8, 8), 8)
-        for n in range(2):
-            near_y[pl.ds(n * 16 + b, 8, stride=2), :] = inv_y[rows, n * 128 : n * 128 + 128]
-    near_high, near_low = cut(jnp.concatenate([near_y[0:16, :], near_y[16:32, :]], axis=1))
-    chosen_high, chosen_low = cut(jnp.concatenate(
-        [
-            inv_xz[pl.ds(pl.multiple_of(side * 128 + (owner // 32) * 16, 16), 16), :]
-            for side in range(2)
-            for owner in owners
-        ],
-        axis=0,
-    ))
     lane = iota((48, 128), 1)
     rows = []
     for px in range(8):
@@ -498,7 +511,6 @@
             held = part if held is None else jnp.where(lane >= iy * 32, part, held)
         rows.append(held)
     high, low = cut(jnp.concatenate(rows, axis=0))
-    ready(3)
     table = fwd_y[...].astype(jnp.bfloat16)
     waves_y = dot(jnp.concatenate([high, low], axis=1), table[0:256]) + dot(high, table[256:384])
     stacked = jnp.concatenate(
@@ -509,11 +521,8 @@
         axis=1,
     )
     high, low = cut(stacked)
-    ready(4)
     table = fwd_xz[...].astype(jnp.bfloat16)
     full = dot(table, jnp.concatenate([high, high], axis=0)) + dot(table[:, 0:128], low)
-    for n in range(5, 8):
-        ready(n)
     slope_x, slope_y, slope_z = spectral[0:128, :], spectral[128:256, :], spectral[256:384, :]
     real, imag = [], []
     for c in range(3):
@@ -531,56 +540,58 @@
 
     cross_real, cross_imag = cross(real), cross(imag)
     high, low = cut(jnp.concatenate([part for c in range(3) for part in (-cross_imag[c], cross_real[c])], axis=1))
+    chosen_high, chosen_low = cut(chosen[...])
     near = dot(jnp.concatenate([chosen_high, chosen_low], axis=1), jnp.concatenate([high, high], axis=0))
     near = near + dot(chosen_high, low)
-    lines = []
-    for c in range(3):
-        low = near[:, c * 256 : c * 256 + 128]
-        high = near[:, c * 256 + 128 : c * 256 + 256]
-        lines.append(jnp.concatenate([low[0:32] - high[32:64], high[0:32] + low[32:64]], axis=1))
-    high, low = cut(jnp.concatenate(lines, axis=0))
-    turned = dot_nt(near_high, high) + (dot_nt(near_high, low) + dot_nt(near_low, high))
-    high, low = cut(jnp.concatenate([turned] * 12, axis=0) * match[...])
+    shares = []
+    for side in range(2):
+        lines = []
+        for c in range(3):
+            low = near[side * 64 : side * 64 + 64, c * 256 : c * 256 + 128]
+            high = near[side * 64 : side * 64 + 64, c * 256 + 128 : c * 256 + 256]
+            lines.append(jnp.concatenate([low[0:32] - high[32:64], high[0:32] + low[32:64]], axis=1))
+        high, low = cut(jnp.concatenate(lines, axis=0))
+        near_high, near_low = cut(jnp.concatenate([near_y[side * 32 + n * 16 : side * 32 + n * 16 + 16, :] for n in range(2)], axis=1))
+        shares.append(dot_nt(near_high, high) + (dot_nt(near_high, low) + dot_nt(near_low, high)))
+    return shares
+
+
+def lift(share, match, spread_z):
+    high, low = cut(jnp.concatenate([share] * 12, axis=0) * match[...])
     table = spread_z[...].astype(jnp.bfloat16)
     return dot(high, table) + dot(low, table)
 
 
-def solve_kernel(owner_ref, *refs):
-    sources, (fresh_out, out_hbm), refs = refs[:11], refs[11:13], refs[13:]
-    held, (near_y, field, moved, sem, out_sem) = refs[:11], refs[11:]
-    loads = [pltpu.make_async_copy(src, dst, sem.at[n]) for n, (src, dst) in enumerate(zip(sources, held))]
+def final_kernel(both_hbm, field_hbm, fresh_hbm, fresh_out, out_hbm, both, field, fresh, moved, sem, out_sem):
+    halves_of = [pl.ds(n * 64, 64) for n in range(2)]
+    loads = [pltpu.make_async_copy(field_hbm, field, sem.at[0])]
+    loads += [pltpu.make_async_copy(both_hbm.at[part], both.at[part], sem.at[1 + n]) for n, part in enumerate(halves_of)]
+    loads += [pltpu.make_async_copy(fresh_hbm, fresh, sem.at[3])]
     for load in loads:
         load.start()
-    base, scale, fresh = held[8:]
-    owners = (owner_ref[0], owner_ref[1])
-    stores = [pltpu.make_async_copy(fresh, fresh_out, out_sem.at[12])]
-
-    def ready(n):
-        loads[n].wait()
-        if n == 7:
-            loads[10].wait()
-            stores[0].start()
-
-    field[...] = solve(owners, ready, *held[:8], near_y)
-    for load in loads[8:10]:
-        load.wait()
-    for ix in range(4):
-        lifted = [[field[(c * 4 + ix) * 16 + h * 8 : (c * 4 + ix) * 16 + h * 8 + 8, :] for h in range(2)] for c in range(3)]
-        for x in range(ix * 8, ix * 8 + 8):
-            for h in range(2):
-                rows = slice(h * 8, h * 8 + 8)
-                part = scale[x, rows, :]
-                for c in range(3):
-                    moved[c * 32 + x, rows, :] = base[c * 32 + x, rows, :] + lifted[c][h] * part
-        for c in range(3):
-            planes = pl.ds(c * 32 + ix * 8, 8)
-            stores.append(pltpu.make_async_copy(moved.at[planes], out_hbm.at[planes], out_sem.at[ix * 3 + c]))
-            stores[-1].start()
+    loads[0].wait()
+    stores = []
+    for n in range(2):
+        loads[1 + n].wait()
+        for ix in (n * 2, n * 2 + 1):
+            lifted = [[field[(c * 4 + ix) * 16 + h * 8 : (c * 4 + ix) * 16 + h * 8 + 8, :] for h in range(2)] for c in range(3)]
+            for x in range(ix * 8, ix * 8 + 8):
+                at = n * 64 + x % 16
+                for h in range(2):
+                    rows = slice(h * 8, h * 8 + 8)
+                    scale = both[at + 48, rows, :]
+                    for c in range(3):
+                        moved[c, x, rows, :] = both[at + c * 16, rows, :] + lifted[c][h] * scale
+        planes = pl.ds(n * 16, 16)
+        stores.append(pltpu.make_async_copy(moved.at[:, planes], out_hbm.at[:, planes], out_sem.at[n]))
+        stores[-1].start()
+    loads[3].wait()
+    stores.append(pltpu.make_async_copy(fresh, fresh_out, out_sem.at[2]))
+    stores[-1].start()
     for copy in stores:
         copy.wait()
 
 
-VMEM = pl.BlockSpec(memory_space=pltpu.VMEM)
 SMEM = pl.BlockSpec(memory_space=pltpu.SMEM)
 ANY = pl.BlockSpec(memory_space=pl.ANY)
 LIMIT = 62 * 2**20
@@ -610,21 +621,17 @@
     def faces(count):
         return [scratch(rows * count, 128) for rows in (96, 192, 96, 96)]
 
-    fresh, base, scale, gathered = pl.pallas_call(
+    sources = (w, u, fish_mask.reshape(256, 128), *(jnp.asarray(a) for a in fold_tables() + solve_tables()))
+    fresh, both, lifted = pl.pallas_call(
         front_kernel,
-        out_shape=(field, field, f32(32, 16, 128), f32(512, 256)),
-        in_specs=[SMEM] * 5 + [ANY] * 6,
-        out_specs=(ANY,) * 4,
+        out_shape=(field, f32(128, 16, 128), f32(192, 128)),
+        in_specs=[SMEM] * 4 + [ANY] * 14,
+        out_specs=(ANY,) * 3,
         scratch_shapes=[
+            *(scratch(*array.shape) for array in sources),
             scratch(96, 16, 128),
-            scratch(96, 16, 128),
-            scratch(256, 128),
-            scratch(128, 256),
-            scratch(192, 256),
-            scratch(8, 192),
-            scratch(96, 16, 128),
-            scratch(96, 16, 128),
-            scratch(32, 16, 128),
+            scratch(128, 16, 128),
+            scratch(192, 128),
             *faces(4),
             *faces(2),
             scratch(192, 128),
@@ -632,33 +639,36 @@
             pltpu.VMEM((64, 128), jnp.int32),
             scratch(192, 128),
             scratch(32, 128),
-            scratch(512, 256),
-            pltpu.SemaphoreType.DMA((6,)),
-            pltpu.SemaphoreType.DMA((5,)),
+            scratch(256, 256),
+            scratch(128, 128),
+            scratch(64, 128),
+            scratch(16, 128),
+            scratch(16, 128),
+            pltpu.SMEM((1,), jnp.int32),
+            pltpu.SemaphoreType.DMA((14,)),
+            pltpu.SemaphoreType.DMA((3,)),
             pltpu.SemaphoreType.DMA((56,)),
             pltpu.SemaphoreType.DMA((56,)),
         ],
         compiler_params=pltpu.CompilerParams(collective_id=0, has_side_effects=True, vmem_limit_bytes=LIMIT),
         name="front",
-    )(neighbours, level_map, patch_owner, fish_slot, fish_speed, w, u, fish_mask.reshape(256, 128),
-      *(jnp.asarray(a) for a in fold_tables()))
-    sources = (gathered, *(jnp.asarray(a) for a in solve_tables()), base, scale, fresh)
+    )(neighbours, level_map, patch_owner, fish_speed, fish_slot, *sources)
     fresh, moved = pl.pallas_call(
-        solve_kernel,
-        out_shape=(field, field),
-        in_specs=[SMEM] + [ANY] * 11,
+        final_kernel,
+        out_shape=(field, f32(3, 32, 16, 128)),
+        in_specs=[ANY] * 3,
         out_specs=(ANY, ANY),
         scratch_shapes=[
-            *(scratch(*array.shape) for array in sources),
-            scratch(32, 128),
+            scratch(128, 16, 128),
             scratch(192, 128),
             scratch(96, 16, 128),
-            pltpu.SemaphoreType.DMA((11,)),
-            pltpu.SemaphoreType.DMA((13,)),
+            scratch(3, 32, 16, 128),
+            pltpu.SemaphoreType.DMA((4,)),
+            pltpu.SemaphoreType.DMA((3,)),
         ],
         compiler_params=pltpu.CompilerParams(vmem_limit_bytes=LIMIT),
-        name="solve",
-    )(patch_owner, *sources)
+        name="final",
+    )(both, lifted, fresh)
     return join(fresh), join(moved)
 
 

time: 50.1 us -> 49 us (0.978)
  Pallas kernels: 48.7 us -> 47.6 us
    pallas_call x2, Pallas kernels: 48.7 us -> 47.6 us  [the longest x1 45.1 us: body(): pl.pallas_call(front_kernel, out_shape=(field, f32(128, 16, 128), f32(192...]
where the time goes in v3:
time: 49 us; the launch traced here: 48.9 us
  Pallas kernels  47.6 us (97%)
  between operations  1.29 us (3%)
    pallas_call x1, Pallas kernels, body(): pl.pallas_call(front_kernel, out_shape=(field, f32(128, 16, 128), f32(192...  45.1 us
    pallas_call x1, Pallas kernels, body(): pl.pallas_call(final_kernel, out_shape=(field, f32(3, 32, 16, 128)), in_s...  2.45 us

profile of v3, /device:TPU:1, one launch (start us, length us, event | category | flops | bytes accessed | tf_op | source)
XLA Modules:
  0.0 48.9 jit_solution(11801966894657989110)
XLA Ops:
  1.3 45.1 %front.1 = (f32[96,16,128]{2,1,0:T(8,128)}, f32[128,16,128]{2,1,0:T(8,128)}, f32[192,128]{1,0:T(8,128)}) custom-call(s32[2,6]{1,0:T(2,128)} %nb_ref.1, s32[2]{0:T(128)} %level_ref.1, s32[2]{0:T(128)} %owner_ref.1, f32[1,3]{1,0:T(1,128)} %speed_ref.1, s32[1]{0:T(128)S(6)} %copy.24.slot_hbm, f32[96,16,128]{2,1,0:T(8,128)} %bitcast.21, ...), custom_call_target="tpu_custom_call" | custom-call | tf_op jit(solution)/shard_map/front/pallas_call | solution.py:625
  46.4 2.4 %final.1 = (f32[96,16,128]{2,1,0:T(8,128)}, f32[3,32,16,128]{3,2,1,0:T(8,128)}) custom-call(f32[128,16,128]{2,1,0:T(8,128)} %get-tuple-element.7.both_hbm, f32[192,128]{1,0:T(8,128)} %get-tuple-element.8.field_hbm, f32[96,16,128]{2,1,0:T(8,128)} %get-tuple-element.9.fresh_hbm), custom_call_target="tpu_custom_call" | custom-call | tf_op jit(solution)/shard_map/final/pallas_call | solution.py:656

commit v4 on v3

--- a/solution.py
+++ b/solution.py
@@ -11,6 +11,9 @@
 
 MESH = pl.DeviceIdType.MESH
 RINGS = 32
+MATES = (2, 3, 4, 5, 6, 7, 1)
+STEPS_Z = (4, 3, 5, 2, 6, 1, 7)
+STEPS_Y = (2, 1, 3)
 GX = 32
 GY = 128
 GZ = 4
@@ -65,16 +68,16 @@
 
 
 def front_kernel(nb_ref, level_ref, owner_ref, speed_ref, slot_hbm, *refs):
-    sources, (fresh_hbm, both_hbm, field_hbm), refs = refs[:13], refs[13:16], refs[16:]
-    held, refs = refs[:13], refs[13:]
-    wv, uv, solid, fold_ref, pick_ref, mean_ref, inv_xz, inv_y, fwd_y, fwd_xz, spectral, match, spread_z = held
-    (out_ref, both, field, s1a, r1a, s2a, r2a, s1b, r1b, s2b, r2b, tmp, nbs, nbr, acc, t1, g, chosen, near_y, mine_s, peer_s,
+    sources, (fresh_hbm, both_hbm, share_hbm), refs = refs[:11], refs[11:14], refs[14:]
+    held, refs = refs[:11], refs[11:]
+    wv, uv, solid, fold_ref, pick_ref, mean_ref, inv_xz, inv_y, fwd_y, fwd_xz, spectral = held
+    (out_ref, both, s1a, r1a, s2a, r2a, s1b, r1b, s2b, r2b, tmp, nbs, nbr, acc, t1, g, chosen, near_y, mine_s, peer_s, share_s,
      slot_ref, in_sem, out_sem, ssem, rsem) = refs
     ring, half, sub = place()
     me = half * 4 + sub
     y, z = ring // 8, lax.rem(ring, 8)
     loads = [pltpu.make_async_copy(src, dst, in_sem.at[n]) for n, (src, dst) in enumerate(zip(sources, held))]
-    loads.append(pltpu.make_async_copy(slot_hbm, slot_ref, in_sem.at[13]))
+    loads.append(pltpu.make_async_copy(slot_hbm, slot_ref, in_sem.at[11]))
     for load in loads:
         load.start()
 
@@ -91,9 +94,9 @@
     def along_y(k):
         return ((lax.rem(y + k, 4) * 8 + z) * 2 + half, sub)
 
-    mates = [mate(k) for k in range(1, 8)]
-    on_z = [along_z(k) for k in range(1, 8)]
-    on_y = [along_y(k) for k in range(1, 4)]
+    mates = [mate(k) for k in MATES]
+    on_z = [along_z(k) for k in STEPS_Z]
+    on_y = [along_y(k) for k in STEPS_Y]
     everyone = mates + [beside(1), beside(-1)] + on_z + on_y
     barrier = pltpu.get_barrier_semaphore()
     for device in everyone:
@@ -136,7 +139,7 @@
     def scatter_faces(part):
         copies = start([
             remote(part.s1.at[part.piece(lax.bitwise_xor(me, k))], part.r1.at[part.piece(4 + me)], part.sem + k - 1, mate(k))
-            for k in range(1, 8)
+            for k in MATES
         ])
         part.r1[part.piece(4 + me), :] = part.s1[part.piece(me), :]
         return copies
@@ -150,7 +153,7 @@
     def return_faces(part):
         copies = start([
             remote(part.s2.at[part.piece(lax.bitwise_xor(me, k))], part.r2.at[part.piece(me)], part.sem + 8 + k, mate(k))
-            for k in range(1, 8)
+            for k in MATES
         ])
         part.r2[part.piece(me), :] = part.s2[part.piece(me), :]
         return copies
@@ -176,7 +179,7 @@
 
     pl.semaphore_wait(barrier, len(everyone))
     mine = pl.ds(pl.multiple_of(me * 8, 8), 8)
-    sent_wants = start([remote(nbs, nbr.at[mine], k - 1, mate(k)) for k in range(1, 8)])
+    sent_wants = start([remote(nbs, nbr.at[mine], k - 1, mate(k)) for k in MATES])
     sent_xy = scatter_faces(xy)
 
     def gather_z(x, held):
@@ -364,7 +367,7 @@
     def share(ref, targets, first):
         return start([remote(ref, ref, first + n, device) for n, device in enumerate(targets)])
 
-    sent = share(t1.at[mine], [mates[k - 1] for k in (2, 4, 6)], 40)
+    sent = share(t1.at[mine], [mate(k) for k in (2, 4, 6)], 40)
 
     on = [jnp.where(slot_ref[0] == b, 10.0, 0.0) for b in range(2)]
     flat_both = both.reshape(2048, 128)
@@ -424,10 +427,10 @@
 
     own, other = solve(g[...], fwd_y, fwd_xz, spectral, chosen, near_y)
     mine_s[:, 0:96] = other
-    sent = start([remote(mine_s, peer_s, 53, mates[0])])
+    sent = start([remote(mine_s, peer_s, 53, mate(1))])
     finish(sent)
-    field[...] = lift(own + peer_s[:, 0:96], match, spread_z)
-    stores += start([pltpu.make_async_copy(field, field_hbm, out_sem.at[2])])
+    share_s[:, 0:96] = own + peer_s[:, 0:96]
+    stores += start([pltpu.make_async_copy(share_s, share_hbm, out_sem.at[2])])
     finish(stores)
 
 
@@ -562,14 +565,18 @@
     return dot(high, table) + dot(low, table)
 
 
-def final_kernel(both_hbm, field_hbm, fresh_hbm, fresh_out, out_hbm, both, field, fresh, moved, sem, out_sem):
+def final_kernel(both_hbm, share_hbm, fresh_hbm, match_hbm, spread_hbm, fresh_out, out_hbm,
+                 both, share, fresh, match, spread_z, field, moved, sem, out_sem):
     halves_of = [pl.ds(n * 64, 64) for n in range(2)]
-    loads = [pltpu.make_async_copy(field_hbm, field, sem.at[0])]
+    loads = [pltpu.make_async_copy(share_hbm, share, sem.at[0])]
     loads += [pltpu.make_async_copy(both_hbm.at[part], both.at[part], sem.at[1 + n]) for n, part in enumerate(halves_of)]
     loads += [pltpu.make_async_copy(fresh_hbm, fresh, sem.at[3])]
-    for load in loads:
+    tables = [pltpu.make_async_copy(match_hbm, match, sem.at[4]), pltpu.make_async_copy(spread_hbm, spread_z, sem.at[5])]
+    for load in loads[:1] + tables + loads[1:]:
         load.start()
-    loads[0].wait()
+    for load in loads[:1] + tables:
+        load.wait()
+    field[...] = lift(share[:, 0:96], match, spread_z)
     stores = []
     for n in range(2):
         loads[1 + n].wait()
@@ -621,17 +628,17 @@
     def faces(count):
         return [scratch(rows * count, 128) for rows in (96, 192, 96, 96)]
 
-    sources = (w, u, fish_mask.reshape(256, 128), *(jnp.asarray(a) for a in fold_tables() + solve_tables()))
-    fresh, both, lifted = pl.pallas_call(
+    *tables, match, spread_z = (jnp.asarray(a) for a in fold_tables() + solve_tables())
+    sources = (w, u, fish_mask.reshape(256, 128), *tables)
+    fresh, both, share = pl.pallas_call(
         front_kernel,
-        out_shape=(field, f32(128, 16, 128), f32(192, 128)),
-        in_specs=[SMEM] * 4 + [ANY] * 14,
+        out_shape=(field, f32(128, 16, 128), f32(16, 128)),
+        in_specs=[SMEM] * 4 + [ANY] * 12,
         out_specs=(ANY,) * 3,
         scratch_shapes=[
             *(scratch(*array.shape) for array in sources),
             scratch(96, 16, 128),
             scratch(128, 16, 128),
-            scratch(192, 128),
             *faces(4),
             *faces(2),
             scratch(192, 128),
@@ -644,8 +651,9 @@
             scratch(64, 128),
             scratch(16, 128),
             scratch(16, 128),
+            scratch(16, 128),
             pltpu.SMEM((1,), jnp.int32),
-            pltpu.SemaphoreType.DMA((14,)),
+            pltpu.SemaphoreType.DMA((12,)),
             pltpu.SemaphoreType.DMA((3,)),
             pltpu.SemaphoreType.DMA((56,)),
             pltpu.SemaphoreType.DMA((56,)),
@@ -656,19 +664,22 @@
     fresh, moved = pl.pallas_call(
         final_kernel,
         out_shape=(field, f32(3, 32, 16, 128)),
-        in_specs=[ANY] * 3,
+        in_specs=[ANY] * 5,
         out_specs=(ANY, ANY),
         scratch_shapes=[
             scratch(128, 16, 128),
+            scratch(16, 128),
+            scratch(96, 16, 128),
+            scratch(192, 96),
+            scratch(96, 128),
             scratch(192, 128),
-            scratch(96, 16, 128),
             scratch(3, 32, 16, 128),
-            pltpu.SemaphoreType.DMA((4,)),
+            pltpu.SemaphoreType.DMA((6,)),
             pltpu.SemaphoreType.DMA((3,)),
         ],
         compiler_params=pltpu.CompilerParams(vmem_limit_bytes=LIMIT),
         name="final",
-    )(both, lifted, fresh)
+    )(both, share, fresh, match, spread_z)
     return join(fresh), join(moved)
 
 

time: 49 us -> 48.4 us (0.988)
  Pallas kernels: 47.6 us -> 47 us
    pallas_call x1, Pallas kernels: 45.1 us -> 44.4 us  [body(): pl.pallas_call(front_kernel, out_shape=(field, f32(128, 16, 128), f32(16,...]
where the time goes in v4:
time: 48.4 us; the launch traced here: 48.2 us
  Pallas kernels  47 us (97%)
  between operations  1.29 us (3%)
    pallas_call x1, Pallas kernels, body(): pl.pallas_call(front_kernel, out_shape=(field, f32(128, 16, 128), f32(16,...  44.4 us
    pallas_call x1, Pallas kernels, body(): pl.pallas_call(final_kernel, out_shape=(field, f32(3, 32, 16, 128)), in_s...  2.51 us

profile of v4, /device:TPU:1, one launch (start us, length us, event | category | flops | bytes accessed | tf_op | source)
XLA Modules:
  0.0 48.2 jit_solution(9118378217760906273)
XLA Ops:
  1.3 44.4 %front.1 = (f32[96,16,128]{2,1,0:T(8,128)}, f32[128,16,128]{2,1,0:T(8,128)}, f32[16,128]{1,0:T(8,128)}) custom-call(s32[2,6]{1,0:T(2,128)} %nb_ref.1, s32[2]{0:T(128)} %level_ref.1, s32[2]{0:T(128)} %owner_ref.1, f32[1,3]{1,0:T(1,128)} %speed_ref.1, s32[1]{0:T(128)S(6)} %copy.24.slot_hbm, f32[96,16,128]{2,1,0:T(8,128)} %bitcast.21, f32[96,16,128]{2,1,0:T(8,128)} %bitcast.22, ...), custom_call_target="tpu_custom_call" | custom-call | tf_op jit(solution)/shard_map/front/pallas_call | solution.py:633
  45.7 2.5 %final.1 = (f32[96,16,128]{2,1,0:T(8,128)}, f32[3,32,16,128]{3,2,1,0:T(8,128)}) custom-call(f32[128,16,128]{2,1,0:T(8,128)} %get-tuple-element.7.both_hbm, f32[16,128]{1,0:T(8,128)} %get-tuple-element.8.share_hbm, f32[96,16,128]{2,1,0:T(8,128)} %get-tuple-element.9.fresh_hbm, f32[192,96]{1,0:T(8,128)} %constant.28.clone.match_hbm, ...), custom_call_target="tpu_custom_call" | custom-call | tf_op jit(solution)/shard_map/final/pallas_call | solution.py:664

commit v5 on v4

--- a/solution.py
+++ b/solution.py
@@ -269,7 +269,7 @@
     planes(23, 31)
     plane(31)
 
-    slot = iota((8, 32), 1)
+    slot = iota((8, 96), 1) & 31
     dead_low = (ring == 0).astype(jnp.int32)
     dead_high = (ring == RINGS - 1).astype(jnp.int32)
     alive = 1 - dead_low * (slot < 8).astype(jnp.int32) - dead_high * (slot >= 24).astype(jnp.int32)
@@ -283,7 +283,7 @@
             data = jnp.concatenate(
                 [part.r1[pl.ds(part.at(0, f ^ 1, c), 32, stride=6 * part.count), :] for c in range(6)], axis=1)
             hot = hot.astype(jnp.bfloat16)
-            got = sum(dot(hot, third) for third in thirds(data))
+            got = dot(hot, jnp.concatenate(thirds(data), axis=0))
             for b in range(2):
                 for c in range(6):
                     part.s2[pl.ds(part.at(b, f, c), 8, stride=part.rows), :] = (

time: 48.4 us -> 48.3 us (level)
  no operation moved by 1% of the time
where the time goes in v5:
time: 48.3 us; the launch traced here: 48.1 us
  Pallas kernels  46.9 us (97%)
  between operations  1.29 us (3%)
    pallas_call x1, Pallas kernels, body(): pl.pallas_call(front_kernel, out_shape=(field, f32(128, 16, 128), f32(16,...  44.4 us
    pallas_call x1, Pallas kernels, body(): pl.pallas_call(final_kernel, out_shape=(field, f32(3, 32, 16, 128)), in_s...  2.51 us

profile of v5, /device:TPU:1, one launch (start us, length us, event | category | flops | bytes accessed | tf_op | source)
XLA Modules:
  0.0 48.1 jit_solution(831559246398743300)
XLA Ops:
  1.3 44.4 %front.1 = (f32[96,16,128]{2,1,0:T(8,128)}, f32[128,16,128]{2,1,0:T(8,128)}, f32[16,128]{1,0:T(8,128)}) custom-call(s32[2,6]{1,0:T(2,128)} %nb_ref.1, s32[2]{0:T(128)} %level_ref.1, s32[2]{0:T(128)} %owner_ref.1, f32[1,3]{1,0:T(1,128)} %speed_ref.1, s32[1]{0:T(128)S(6)} %copy.24.slot_hbm, f32[96,16,128]{2,1,0:T(8,128)} %bitcast.21, f32[96,16,128]{2,1,0:T(8,128)} %bitcast.22, ...), custom_call_target="tpu_custom_call" | custom-call | tf_op jit(solution)/shard_map/front/pallas_call | solution.py:633
  45.6 2.5 %final.1 = (f32[96,16,128]{2,1,0:T(8,128)}, f32[3,32,16,128]{3,2,1,0:T(8,128)}) custom-call(f32[128,16,128]{2,1,0:T(8,128)} %get-tuple-element.7.both_hbm, f32[16,128]{1,0:T(8,128)} %get-tuple-element.8.share_hbm, f32[96,16,128]{2,1,0:T(8,128)} %get-tuple-element.9.fresh_hbm, f32[192,96]{1,0:T(8,128)} %constant.28.clone.match_hbm, ...), custom_call_target="tpu_custom_call" | custom-call | tf_op jit(solution)/shard_map/final/pallas_call | solution.py:664

commit v6 on v5

--- a/solution.py
+++ b/solution.py
@@ -129,9 +129,17 @@
             copy.start()
         return copies
 
+    leaving = []
+
     def finish(copies):
         for copy in copies:
-            copy.wait()
+            copy.wait_recv()
+        leaving.extend(copies)
+
+    def drain():
+        for copy in leaving:
+            copy.wait_send()
+        leaving.clear()
 
     xy = Chunk(0, 4, s1a, r1a, s2a, r2a, 8)
     zz = Chunk(4, 2, s1b, r1b, s2b, r2b, 24)
@@ -369,6 +377,8 @@
 
     sent = share(t1.at[mine], [mate(k) for k in (2, 4, 6)], 40)
 
+    drain()
+
     on = [jnp.where(slot_ref[0] == b, 10.0, 0.0) for b in range(2)]
     flat_both = both.reshape(2048, 128)
 
@@ -395,6 +405,8 @@
         g[at, t * 128 : t * 128 + 128] = t1[pl.ds(t, 8, stride=4), :]
     sent = share(g.at[at], on_z, 43)
 
+    drain()
+
     theirs = nbr[pl.ds(pl.multiple_of(lax.bitwise_xor(me, 1) * 8, 8), 8), :]
     owners = [jnp.full((8, 128), owner_ref[b], jnp.int32) for b in range(2)]
     owners += [jnp.broadcast_to(theirs[:, 12 + b : 13 + b], (8, 128)) for b in range(2)]
@@ -431,7 +443,9 @@
     finish(sent)
     share_s[:, 0:96] = own + peer_s[:, 0:96]
     stores += start([pltpu.make_async_copy(share_s, share_hbm, out_sem.at[2])])
-    finish(stores)
+    drain()
+    for copy in stores:
+        copy.wait()
 
 
 def halves(table):

time: 48.3 us -> 48.3 us (level)
  no operation moved by 1% of the time
where the time goes in v6:
time: 48.3 us; the launch traced here: 48.1 us
  Pallas kernels  46.8 us (97%)
  between operations  1.29 us (3%)
    pallas_call x1, Pallas kernels, body(): pl.pallas_call(front_kernel, out_shape=(field, f32(128, 16, 128), f32(16,...  44.3 us
    pallas_call x1, Pallas kernels, body(): pl.pallas_call(final_kernel, out_shape=(field, f32(3, 32, 16, 128)), in_s...  2.51 us

profile of v6, /device:TPU:1, one launch (start us, length us, event | category | flops | bytes accessed | tf_op | source)
XLA Modules:
  0.0 48.1 jit_solution(12674399822376200839)
XLA Ops:
  1.3 44.3 %front.1 = (f32[96,16,128]{2,1,0:T(8,128)}, f32[128,16,128]{2,1,0:T(8,128)}, f32[16,128]{1,0:T(8,128)}) custom-call(s32[2,6]{1,0:T(2,128)} %nb_ref.1, s32[2]{0:T(128)} %level_ref.1, s32[2]{0:T(128)} %owner_ref.1, f32[1,3]{1,0:T(1,128)} %speed_ref.1, s32[1]{0:T(128)S(6)} %copy.24.slot_hbm, f32[96,16,128]{2,1,0:T(8,128)} %bitcast.21, f32[96,16,128]{2,1,0:T(8,128)} %bitcast.22, ...), custom_call_target="tpu_custom_call" | custom-call | tf_op jit(solution)/shard_map/front/pallas_call | solution.py:647
  45.6 2.5 %final.1 = (f32[96,16,128]{2,1,0:T(8,128)}, f32[3,32,16,128]{3,2,1,0:T(8,128)}) custom-call(f32[128,16,128]{2,1,0:T(8,128)} %get-tuple-element.7.both_hbm, f32[16,128]{1,0:T(8,128)} %get-tuple-element.8.share_hbm, f32[96,16,128]{2,1,0:T(8,128)} %get-tuple-element.9.fresh_hbm, f32[192,96]{1,0:T(8,128)} %constant.28.clone.match_hbm, ...), custom_call_target="tpu_custom_call" | custom-call | tf_op jit(solution)/shard_map/final/pallas_call | solution.py:678
